TPU v7x, 512 devices: a whole 4x4x16 slice. The times are simulated.
512 devices in a mesh: dp: 4 (over x), ctx: 16 (over z), tp: 8 (over y, core).
Axes of the slice: x: 4, y: 4, z: 16, core: 2. Of those that a mesh axis runs over, the one named last changes fastest.
Arguments:
- inputs: bfloat16 [4, 4096, 8192], P('dp', 'ctx', 'tp'), may hold values from -6 to 6
- cotangent: bfloat16 [4, 4096, 8192], P('dp', 'ctx', 'tp'), may hold values from -6 to 6
- residues: float32 [512, 16], P('tp'), may hold values from -3 to 3
- decay_rates: float32 [512, 16], P('tp'), may hold values from 4.8828125e-05 to 0.0333333333
- skip_gain: float32 [8192], P('tp'), may hold values from -1 to 1
Outputs:
- outputs: bfloat16 [4, 4096, 8192], P('dp', 'ctx', 'tp')
- grad_inputs: bfloat16 [4, 4096, 8192], P('dp', 'ctx', 'tp')
- grad_residues: float32 [512, 16], P('tp')
- grad_skip: float32 [8192], P('tp')
All inputs are finite; a program needn't handle non-finite values.
Results may differ from a plain program's by a relative error of at most 0.0014.
Values sent between devices are 32-bit elements; how exact they have to be, the bound alone decides.
A program may use at most 64 MiB of HBM per device.

v0:
```python
import math

import jax
import jax.numpy as jnp
from jax import lax
from jax.sharding import PartitionSpec as P

highest = lax.Precision.HIGHEST


def passed_along(value, axis, by):
    length = lax.axis_size(axis)
    pairs = [(i, i + by) for i in range(length) if 0 <= i + by < length]
    return lax.ppermute(value, axis, pairs)


def shards(inputs, cotangent, residues, decay_rates, skip_gain):
    local_batch, block_rows, channels = inputs.shape
    group_count, mode_count = residues.shape
    group_width = channels // group_count
    sub_rows = math.gcd(256, block_rows)
    sub_count = block_rows // sub_rows
    weight = jnp.sqrt(1.0 - jnp.exp(-2.0 * decay_rates))
    coefficient = residues * weight
    positions = jnp.arange(sub_rows, dtype=jnp.float32)
    center = (sub_rows - 1) / 2.0
    rate_cube = decay_rates[:, :, None]
    decay_down = jnp.exp(-rate_cube * (positions - center))
    decay_up = jnp.exp(rate_cube * (positions - center))
    from_start = jnp.exp(-rate_cube * positions)
    to_end = jnp.exp(-rate_cube * (sub_rows - 1.0 - positions))
    five_shape = (local_batch, sub_count, sub_rows, group_count, group_width)
    state_shape = (local_batch, mode_count, channels)
    state_split = (local_batch, mode_count, group_count, group_width)
    inputs_wide = inputs.astype(jnp.float32).reshape(five_shape)
    cotangent_wide = cotangent.astype(jnp.float32).reshape(five_shape)
    sub_ends = jnp.einsum("gmt,bktgc->kbmgc", to_end, inputs_wide, precision=highest)
    sub_starts = jnp.einsum("gmt,bktgc->kbmgc", from_start, cotangent_wide, precision=highest)
    device_end = sub_ends[0]
    device_start = sub_starts[sub_count - 1]
    end_states = device_end.reshape(state_shape)
    start_states = device_start.reshape(state_shape)
    channel_rates = jnp.repeat(decay_rates.T, group_width, axis=1) * float(block_rows)
    passing = jnp.exp(-channel_rates)

    def relay_turn(turn, carried):
        incoming_x, incoming_d = carried
        sent_x = incoming_x * passing + end_states
        sent_d = incoming_d * passing + start_states
        return (passed_along(sent_x, "ctx", 1), passed_along(sent_d, "ctx", -1))

    empty_states = jnp.zeros_like(end_states)
    state_before, state_after = lax.fori_loop(
        0, lax.axis_size("ctx") - 1, relay_turn, (empty_states, empty_states)
    )
    block_count = math.gcd(group_count, 16)
    per_block = group_count // block_count
    causal_mask = positions[:, None] >= positions[None, :]

    def by_groups(array):
        return array.reshape((block_count, per_block) + array.shape[1:])

    def data_blocks(array):
        return array.reshape(
            local_batch, sub_count, sub_rows, block_count, per_block, group_width
        ).transpose(3, 0, 1, 2, 4, 5)

    def local_block(pieces):
        coef_piece, down_piece, up_piece, weight_piece, wide_x, wide_d, half_x, half_d = pieces
        kernel = jnp.where(
            causal_mask,
            jnp.einsum("gm,gmt,gms->gts", coef_piece, down_piece, up_piece, precision=highest),
            0.0,
        )
        local_out = jnp.einsum("gts,bksgc->bktgc", kernel, wide_x, precision=highest)
        local_back = jnp.einsum("gts,bktgc->bksgc", kernel, wide_d, precision=highest)
        pairs = jnp.einsum("bktgc,bksgc->gts", half_d, half_x, preferred_element_type=jnp.float32)
        pairs = jnp.where(causal_mask, pairs, 0.0)
        local_grad = weight_piece * jnp.einsum(
            "gmt,gts,gms->gm", down_piece, pairs, up_piece, precision=highest
        )
        return (local_out, local_back, local_grad)

    half_inputs = inputs.reshape(five_shape)
    half_cotangent = cotangent.reshape(five_shape)
    block_out, block_back, block_grad = lax.map(
        local_block,
        (
            by_groups(coefficient),
            by_groups(decay_down),
            by_groups(decay_up),
            by_groups(weight),
            data_blocks(inputs_wide),
            data_blocks(cotangent_wide),
            data_blocks(half_inputs),
            data_blocks(half_cotangent),
        ),
    )
    local_out = block_out.transpose(1, 2, 3, 0, 4, 5).reshape(five_shape)
    local_back = block_back.transpose(1, 2, 3, 0, 4, 5).reshape(five_shape)
    local_grad = block_grad.reshape(group_count, mode_count)
    running = state_before.reshape(state_split)
    before_list = [running]
    running = state_after.reshape(state_split)
    after_list = [None] * sub_count
    after_list[0] = running
    before_stack = jnp.stack(before_list, axis=1)
    after_stack = jnp.stack(after_list, axis=1)
    first_weights = coefficient[:, :, None] * jnp.exp(-rate_cube * (positions + 1.0))
    last_weights = coefficient[:, :, None] * jnp.exp(-rate_cube * (sub_rows - positions))
    carried_out = jnp.einsum("gmt,bkmgc->bktgc", first_weights, before_stack, precision=highest)
    carried_back = jnp.einsum("gmt,bkmgc->bktgc", last_weights, after_stack, precision=highest)
    carried_grad = (
        weight
        * jnp.exp(-decay_rates)
        * jnp.einsum("kbmgc,bkmgc->gm", sub_starts, before_stack, precision=highest)
    )
    skip_wide = skip_gain.reshape(group_count, group_width)
    outputs = (
        (local_out + carried_out + skip_wide * inputs_wide)
        .reshape(local_batch, block_rows, channels)
        .astype(jnp.bfloat16)
    )
    grad_inputs = (
        (local_back + carried_back + skip_wide * cotangent_wide)
        .reshape(local_batch, block_rows, channels)
        .astype(jnp.bfloat16)
    )
    token_total = local_batch * block_rows * lax.axis_size("dp") * lax.axis_size("ctx")
    scale = 1.0 / math.sqrt(token_total)
    skip_local = jnp.sum(inputs_wide * cotangent_wide, axis=(0, 1, 2)).reshape(channels)
    grad_residues, grad_skip = lax.psum(
        ((local_grad + carried_grad) * scale, skip_local * scale), ("dp", "ctx")
    )
    return (outputs, grad_inputs, grad_residues, grad_skip)


def solution(mesh):
    placed = (P("dp", "ctx", "tp"), P("dp", "ctx", "tp"), P("tp", None), P("tp", None), P("tp"))
    return jax.shard_map(
        shards,
        mesh=mesh,
        in_specs=placed,
        out_specs=(P("dp", "ctx", "tp"), P("dp", "ctx", "tp"), P("tp", None), P("tp")),
        check_vma=False,
    )
```

profile of v0, /device:TPU:24, one launch (start us, length us, event | category | flops | bytes accessed | tf_op | source)
XLA Modules:
  0.0 629.1 jit_solution(2040821487755064121)
XLA Ops:
  6.7 172.4 %while.30 = (s32[]{:T(128)}, f32[16,1,1,256,4,16]{3,5,4,2,1,0:T(8,128)}, f32[16,1,1,256,4,16]{3,5,4,2,1,0:T(8,128)}, f32[16,4,16]{2,1,0:T(4,128)S(1)}, f32[16,1,...) while((s32[]{:T(128)}, ...), condition=%wide.region_1.0_spmd.clone.clone, body=%wide.region_0.0_spmd.clone.clone.sunk | while | flops 210354176 | bytes 6303369 | solution.py:86
  184.8 158.3 %while.29 = (s32[]{:T(128)}, f32[1,16,1024]{2,1,0:T(8,128)S(1)}, f32[1,16,1024]{2,1,0:T(8,128)S(1)}, f32[1,16,1024]{2,1,0:T(8,128)S(1)}, f32[1,16,1024]{2,1,0:T(8,128)S(1)}, /*index=5*/f32[16,64]{1,0:T(8,128)S(1)}, s32[]{:T(128)}) while((s32[]{:T(128)}, f32[1,16,1024]{2,1,0:T(8,128)S(1)}, f32[1,16,1024]{2,1,0:T(8,128)S(1)}, ...), condition=%wide.region_3.4_spmd.clone, body=%wide.region_2.3_spmd.clone.sunk | while | flops 65538 | bytes 1183901 | solution.py:53
  191.0 4.3 collective-permute-done.1
  201.5 5.3 collective-permute-done.1
  207.3 5.1 collective-permute-start
  214.3 4.3 collective-permute-done.1
  219.1 3.9 collective-permute-start
  224.9 4.3 collective-permute-done.1
  229.7 4.8 collective-permute-start
  236.3 4.3 collective-permute-done.1
  241.1 5.1 collective-permute-start
  248.1 4.3 collective-permute-done.1
  252.9 3.9 collective-permute-start
  259.0 4.4 collective-permute-done.1
  263.9 3.9 collective-permute-start
  269.7 4.3 collective-permute-done.1
  279.2 4.3 collective-permute-done.1
  289.2 4.3 collective-permute-done.1
  299.0 4.3 collective-permute-done.1
  308.9 4.3 collective-permute-done.1
  319.1 4.6 collective-permute-done.1
  329.5 4.3 collective-permute-done.1
  338.9 4.3 collective-permute-done.1
  353.2 275.2 %all-reduce = (f32[64,16]{1,0:T(8,128)S(1)}, f32[1024]{0:T(1024)}) all-reduce(f32[64,16]{1,0:T(8,128)S(1)} %add_multiply_fusion, f32[1024]{0:T(1024)S(1)} %broadcast_multiply_fusion), channel_id=1, replica_groups=mesh['dp'=4,'ctx'=16,'tp'=8] {'dp','ctx'}, use_global_device_ids=true, to_apply=%region_4.5 | all-reduce | flops 2048 | bytes 16384 | tf_op jit(solution)/shard_map/psum | solution.py:132
  (297 shorter events, 259.3 us)
Async XLA Ops:
  185.3 5.7 collective-permute-start
  189.1 6.2 collective-permute-start.1
  195.8 5.7 collective-permute-start
  199.6 7.2 %collective-permute-start.1 = (f32[1,16,1024]{2,1,0:T(8,128)S(1)}, f32[1,16,1024]{2,1,0:T(8,128)S(1)}, u32[]{:S(2)}, u32[]{:S(2)}) collective-permute-start(f32[1,16,1024]{2,1,0:T(8,128)S(1)} %get-tuple-element.351), channel_id=1, source_target_pairs={{8,0},{16,8},{24,16},{32,24},{40,32},{48,40},{56,48},{64,56},{72,6... | collective-permute-start | bytes 196616 | tf_op jit(solution)/shard_map/while/body/eval_jaxpr/ppermute | solution.py:14
  207.3 7.0 %collective-permute-start = (f32[1,16,1024]{2,1,0:T(8,128)S(1)}, f32[1,16,1024]{2,1,0:T(8,128)S(1)}, u32[]{:S(2)}, u32[]{:S(2)}) collective-permute-start(f32[1,16,1024]{2,1,0:T(8,128)S(1)} %get-tuple-element.350), channel_id=1, source_target_pairs={{0,8},{8,16},{16,24},{24,32},{32,40},{40,48},{48,56},{56,64},{64,7... | collective-permute-start | bytes 196616 | tf_op jit(solution)/shard_map/while/body/eval_jaxpr/ppermute | solution.py:14
  212.4 6.2 collective-permute-start.1
  219.1 5.8 collective-permute-start
  223.0 6.2 collective-permute-start.1
  229.7 6.6 %collective-permute-start = (f32[1,16,1024]{2,1,0:T(8,128)S(1)}, f32[1,16,1024]{2,1,0:T(8,128)S(1)}, u32[]{:S(2)}, u32[]{:S(2)}) collective-permute-start(f32[1,16,1024]{2,1,0:T(8,128)S(1)} %get-tuple-element.350), channel_id=1, source_target_pairs={{0,8},{8,16},{16,24},{24,32},{32,40},{40,48},{48,56},{56,64},{64,7... | collective-permute-start | bytes 196616 | tf_op jit(solution)/shard_map/while/body/eval_jaxpr/ppermute | solution.py:14
  234.4 6.2 collective-permute-start.1
  241.1 7.0 %collective-permute-start = (f32[1,16,1024]{2,1,0:T(8,128)S(1)}, f32[1,16,1024]{2,1,0:T(8,128)S(1)}, u32[]{:S(2)}, u32[]{:S(2)}) collective-permute-start(f32[1,16,1024]{2,1,0:T(8,128)S(1)} %get-tuple-element.350), channel_id=1, source_target_pairs={{0,8},{8,16},{16,24},{24,32},{32,40},{40,48},{48,56},{56,64},{64,7... | collective-permute-start | bytes 196616 | tf_op jit(solution)/shard_map/while/body/eval_jaxpr/ppermute | solution.py:14
  246.2 6.2 collective-permute-start.1
  252.9 6.1 collective-permute-start
  256.8 6.6 %collective-permute-start.1 = (f32[1,16,1024]{2,1,0:T(8,128)S(1)}, f32[1,16,1024]{2,1,0:T(8,128)S(1)}, u32[]{:S(2)}, u32[]{:S(2)}) collective-permute-start(f32[1,16,1024]{2,1,0:T(8,128)S(1)} %get-tuple-element.351), channel_id=1, source_target_pairs={{8,0},{16,8},{24,16},{32,24},{40,32},{48,40},{56,48},{64,56},{72,6... | collective-permute-start | bytes 196616 | tf_op jit(solution)/shard_map/while/body/eval_jaxpr/ppermute | solution.py:14
  263.9 5.8 collective-permute-start
  267.8 6.2 collective-permute-start.1
  277.3 6.2 collective-permute-start.1
  287.3 6.2 collective-permute-start.1
  297.1 6.2 collective-permute-start.1
  307.0 6.2 collective-permute-start.1
  313.7 5.4 collective-permute-start
  317.1 6.5 %collective-permute-start.1 = (f32[1,16,1024]{2,1,0:T(8,128)S(1)}, f32[1,16,1024]{2,1,0:T(8,128)S(1)}, u32[]{:S(2)}, u32[]{:S(2)}) collective-permute-start(f32[1,16,1024]{2,1,0:T(8,128)S(1)} %get-tuple-element.351), channel_id=1, source_target_pairs={{8,0},{16,8},{24,16},{32,24},{40,32},{48,40},{56,48},{64,56},{72,6... | collective-permute-start | bytes 196616 | tf_op jit(solution)/shard_map/while/body/eval_jaxpr/ppermute | solution.py:14
  327.6 6.2 collective-permute-start.1
  337.0 6.2 collective-permute-start.1
  (14 other events, 38.0 us)
where the time goes:
time: 634 us; the launch traced here: 629 us
  blocking collectives  275 us (43%)
  matrix products  163 us (26%)
  starting transfers between devices  75.9 us (12%)
  waiting for transfers between devices  74.7 us (12%)
  local copies, waits for them, and re-layouts  34.5 us (5%)
    psum x1, blocking collectives, shards(): lax.psum(((local_grad + carried_grad) * scale, skip_local * scale), ('dp'...  275 us
    ppermute x30, starting transfers between devices, passed_along(): return lax.ppermute(value, axis, pairs)  75.9 us
    ppermute x30, waiting for transfers between devices, passed_along(): return lax.ppermute(value, axis, pairs)  74.7 us
    dot_general x16, matrix products, local_block(): jnp.einsum('gmt,gts,gms->gm', down_piece, pairs, up_piece, precision=high...  43.6 us
    dot_general x16, matrix products, local_block(): jnp.einsum('gts,bksgc->bktgc', kernel, wide_x, precision=highest)  39.2 us
    dot_general x16, matrix products, local_block(): jnp.einsum('gm,gmt,gms->gts', coef_piece, down_piece, up_piece, precision...  32.7 us
    dot_general x16, matrix products, local_block(): jnp.einsum('gts,bktgc->bksgc', kernel, wide_d, precision=highest)  19.9 us
    dot_general x16, matrix products, local_block(): jnp.einsum('bktgc,bksgc->gts', half_d, half_x, preferred_element_type=jnp...  17.8 us
  transfers between devices with their start and end apart: 30, of which 30 were waited for; matrix products, arithmetic and copies ran while one was open for 0% of the time, Pallas kernels for 0%

commit v1 on v0

v1 whole, which is shorter than its diff:
```python
import functools
import math

import jax
import jax.numpy as jnp
import numpy as np
from jax import lax
from jax.experimental import pallas as pl
from jax.experimental.pallas import tpu as pltpu
from jax.sharding import PartitionSpec as P

MESH = pl.DeviceIdType.MESH
highest = lax.Precision.HIGHEST
f32 = jnp.float32
bf16 = jnp.bfloat16


def split(value):
    high = value.astype(bf16)
    return high, (value - high.astype(f32)).astype(bf16)


def times(left, right):
    total = jnp.dot(left[0], right[0], preferred_element_type=f32)
    total += jnp.dot(left[0], right[1], preferred_element_type=f32)
    return total + jnp.dot(left[1], right[0], preferred_element_type=f32)


def kernel(sizes, x_hbm, d_hbm, res_hbm, rate_hbm, skip_hbm, fwd_hbm, inv_hbm, trig_hbm,
           y_ref, z_ref, gres_ref, gskip_ref,
           x_ref, d_ref, res_ref, rate_ref, skip_ref, fwd_ref, inv_ref, trig_ref,
           wf_ref, wb_ref, h_ref, ylocal, zlocal, states, coefs, packs, e_send, e_recv, s_send, s_recv,
           g_send, g_recv, p_send, p_recv, o_send, o_recv, load_sem, send_sem, recv_sem, psend_sem, precv_sem):
    nctx, ndp, rows, channels, groups, modes, scale = sizes
    half = rows // 2
    tiles = channels // 256
    me = lax.axis_index("ctx")
    mine = lax.axis_index("dp")

    barrier = pltpu.get_barrier_semaphore()

    def greet(step, carried):
        pl.semaphore_signal(barrier, inc=1, device_id={"ctx": lax.rem(me + step, nctx)}, device_id_type=MESH)
        return carried

    lax.fori_loop(1, nctx, greet, 0)
    for step in range(1, ndp):
        pl.semaphore_signal(barrier, inc=1, device_id={"dp": lax.rem(mine + step, ndp)}, device_id_type=MESH)

    loads = [
        pltpu.make_async_copy(source, target, load_sem.at[number])
        for number, (source, target) in enumerate(
            [(rate_hbm, rate_ref), (res_hbm, res_ref), (x_hbm.at[0], x_ref), (d_hbm.at[0], d_ref), (trig_hbm, trig_ref),
             (fwd_hbm, fwd_ref), (inv_hbm, inv_ref), (skip_hbm, skip_ref)]
        )
    ]
    for load in loads:
        load.start()

    block_ones = lax.broadcasted_iota(jnp.int32, (256, 256), 0) // modes == lax.broadcasted_iota(jnp.int32, (256, 256), 1) // modes
    ones = block_ones.astype(bf16)
    lanes = lax.broadcasted_iota(jnp.int32, (8, 128), 1)
    lower = lanes < 64
    lower_row = lax.broadcasted_iota(jnp.int32, (1, 128), 1) < 64
    positions = lax.broadcasted_iota(jnp.int32, (rows, 1), 0).astype(f32)

    spread = (
        lax.broadcasted_iota(jnp.int32, (modes, channels), 1) % modes == lax.broadcasted_iota(jnp.int32, (modes, channels), 0)
    ).astype(f32)
    own_group = (
        lax.broadcasted_iota(jnp.int32, (groups, channels), 1) // modes == lax.broadcasted_iota(jnp.int32, (groups, channels), 0)
    )
    own_mode = (
        lax.broadcasted_iota(jnp.int32, (modes, channels), 1) % modes == lax.broadcasted_iota(jnp.int32, (modes, channels), 0)
    )

    def as_row(array):
        wide = jnp.dot(array, spread, precision=highest, preferred_element_type=f32)
        return jnp.sum(jnp.where(own_group, wide, 0.0), axis=0, keepdims=True)

    def by_channel(row):
        wide = jnp.where(own_mode, row, 0.0)
        return jnp.concatenate(
            [
                jnp.dot(wide[:, 256 * q : 256 * q + 256], ones.astype(f32), precision=highest, preferred_element_type=f32)
                for q in range(tiles)
            ],
            axis=1,
        )

    def pack(array, target):
        for pair in range(nctx // 2):
            low = array[0:8, 128 * pair : 128 * pair + 128]
            high = array[8:16, 128 * pair : 128 * pair + 128]
            target[2 * pair] = jnp.where(lower, low, pltpu.roll(high, 64, 1))
            target[2 * pair + 1] = jnp.where(lower, pltpu.roll(low, 64, 1), high)

    def unpack(source):
        lows, highs = [], []
        for pair in range(nctx // 2):
            first, second = source[2 * pair], source[2 * pair + 1]
            lows.append(jnp.where(lower, first, pltpu.roll(second, 64, 1)))
            highs.append(jnp.where(lower, pltpu.roll(first, 64, 1), second))
        return jnp.concatenate([jnp.concatenate(lows, axis=1), jnp.concatenate(highs, axis=1)], axis=0)

    def on_blocks(array, q):
        piece = array[:, 256 * q : 256 * q + 256]
        return jnp.where(block_ones, jnp.concatenate([piece] * (256 // modes), axis=0), 0.0)

    def off_blocks(array):
        return jnp.sum(jnp.where(block_ones, array, 0.0).reshape(256 // modes, modes, 256), axis=0)

    def transposed_dot(left, right):
        return lax.dot_general(left, right, (((0,), (0,)), ((), ())), preferred_element_type=f32)

    loads[0].wait()
    rate_row = as_row(rate_ref[...])
    for q in range(tiles):
        piece = slice(256 * q, 256 * q + 256)
        rate_piece = rate_row[:, piece]
        high, low = split(jnp.exp(-rate_piece * (rows - 1.0 - positions)))
        wb_ref[0, :, piece] = high
        wb_ref[1, :, piece] = low
    loads[2].wait()
    for q in range(tiles):
        piece = slice(256 * q, 256 * q + 256)
        full = transposed_dot(wb_ref[0, :, piece], x_ref[:, piece]) + transposed_dot(wb_ref[1, :, piece], x_ref[:, piece])
        states[0, :, piece] = off_blocks(full)
    pack(states[0], e_send)
    for q in range(tiles):
        piece = slice(256 * q, 256 * q + 256)
        high, low = split(jnp.exp(-rate_row[:, piece] * positions))
        wf_ref[0, :, piece] = high
        wf_ref[1, :, piece] = low
    loads[3].wait()
    for q in range(tiles):
        piece = slice(256 * q, 256 * q + 256)
        full = transposed_dot(wf_ref[0, :, piece], d_ref[:, piece]) + transposed_dot(wf_ref[1, :, piece], d_ref[:, piece])
        states[1, :, piece] = off_blocks(full)
    pack(states[1], s_send)

    def copy_to(step, kind, send, recv, slot_there, slot_here):
        there = lax.rem(me + step, nctx)
        return pltpu.make_async_remote_copy(
            src_ref=send.at[there] if slot_here else send,
            dst_ref=recv.at[me],
            send_sem=send_sem.at[kind, there],
            recv_sem=recv_sem.at[kind, me],
            device_id={"ctx": there},
            device_id_type=MESH,
        )

    def arrival(step, kind, send, recv, slot_here):
        origin = lax.rem(me + step, nctx)
        return pltpu.make_async_remote_copy(
            src_ref=send.at[origin] if slot_here else send,
            dst_ref=recv.at[origin],
            send_sem=send_sem.at[kind, origin],
            recv_sem=recv_sem.at[kind, origin],
            device_id={"ctx": origin},
            device_id_type=MESH,
        )

    def send_all(kind, send, recv, slot_here=True):
        def one(turn, carried):
            step = nctx // 2 + jnp.where(turn % 2 == 1, -((turn + 1) // 2), turn // 2)
            copy_to(step, kind, send, recv, None, slot_here).start()
            return carried

        lax.fori_loop(0, nctx - 1, one, 0)

    def await_all(kind, send, recv, slot_here=True):
        def one(step, carried):
            arrival(step, kind, send, recv, slot_here).wait_recv()
            return carried

        lax.fori_loop(1, nctx, one, 0)

    def await_sent(kind, send, recv, slot_here=True):
        def one(step, carried):
            arrival(step, kind, send, recv, slot_here).wait_send()
            return carried

        lax.fori_loop(1, nctx, one, 0)

    pl.semaphore_wait(barrier, nctx - 1 + ndp - 1)
    send_all(0, e_send, e_recv.at[0])
    send_all(1, s_send, s_recv.at[0])
    e_recv[0, me] = e_send[me]
    s_recv[0, me] = s_send[me]

    loads[1].wait()
    weight_row = jnp.sqrt(1.0 - jnp.exp(-2.0 * rate_row))
    step_row = jnp.exp(-rate_row)
    coef = by_channel(as_row(res_ref[...]) * weight_row)
    rate_wide = by_channel(rate_row)
    step_wide = jnp.exp(-rate_wide)
    block_wide = jnp.exp(-rate_wide * float(rows))
    inverse_wide = 1.0 / (1.0 + block_wide)
    coefs[0] = coef * step_wide
    coefs[1] = inverse_wide
    pack(block_wide, packs.at[0])
    pack(inverse_wide, packs.at[1])
    pack(step_wide, packs.at[2])
    loads[4].wait()
    loads[5].wait()
    loads[6].wait()
    loads[7].wait()
    less_cos, sine = trig_ref[:, 0:1], trig_ref[:, 1:2]
    for q in range(tiles):
        piece = slice(256 * q, 256 * q + 256)
        step_piece = step_row[:, piece]
        rest = 1.0 - step_piece
        near = step_piece * less_cos
        below = 1.0 / (rest * rest + 2.0 * near)
        real, imag = (rest + near) * below, (-step_piece * sine) * below
        h_ref[0:half] = real
        h_ref[half:rows] = imag
        response = times(split(h_ref[...]), split(on_blocks(coef, q)))
        f_re, f_im = response[0:half], response[half:rows]
        x_piece, d_piece = x_ref[:, piece], d_ref[:, piece]
        x_hat = jnp.dot(fwd_ref[0], x_piece, preferred_element_type=f32) + jnp.dot(fwd_ref[1], x_piece, preferred_element_type=f32)
        d_hat = jnp.dot(fwd_ref[0], d_piece, preferred_element_type=f32) + jnp.dot(fwd_ref[1], d_piece, preferred_element_type=f32)
        x_re, x_im, d_re, d_im = x_hat[0:half], x_hat[half:rows], d_hat[0:half], d_hat[half:rows]
        skip = skip_ref[:, piece]
        x_wide, d_wide = x_piece.astype(f32), d_piece.astype(f32)
        y_hat = jnp.concatenate([f_re * x_re - f_im * x_im, f_re * x_im + f_im * x_re], axis=0)
        ylocal[:, piece] = times((inv_ref[0], inv_ref[1]), split(y_hat)) + skip * x_wide
        z_hat = jnp.concatenate([f_re * d_re + f_im * d_im, f_re * d_im - f_im * d_re], axis=0)
        zlocal[:, piece] = times((inv_ref[0], inv_ref[1]), split(z_hat)) + skip * d_wide
        cross = jnp.concatenate([d_re * x_re + d_im * x_im, d_im * x_re - d_re * x_im], axis=0)
        cross_high, cross_low = split(cross)
        grouped = jnp.dot(cross_high, ones, preferred_element_type=f32) + jnp.dot(cross_low, ones, preferred_element_type=f32)
        grad_piece = jnp.sum(grouped * h_ref[...], axis=0, keepdims=True) * (2.0 / rows)
        skip_piece = jnp.sum(x_wide * d_wide, axis=0, keepdims=True)
        for part in range(2):
            pair = 2 * q + part
            grad_row, skip_row = grad_piece[:, 128 * part : 128 * part + 128], skip_piece[:, 128 * part : 128 * part + 128]
            g_send[2 * pair] = jnp.where(lower_row, grad_row, pltpu.roll(skip_row, 64, 1))
            g_send[2 * pair + 1] = jnp.where(lower_row, pltpu.roll(grad_row, 64, 1), skip_row)
    send_all(2, g_send, g_recv)
    g_recv[me] = g_send[me]

    block_own, inverse_own, step_own = packs[0, me], packs[1, me], packs[2, me]
    await_all(0, e_send, e_recv.at[0])
    running = jnp.zeros((8, 128), f32)
    for block in range(nctx):
        e_recv[1, block] = running
        running = running * block_own + e_recv[0, block]
    send_all(3, e_recv.at[1], p_recv.at[0])
    p_recv[0, me] = e_recv[1, me]
    await_all(1, s_send, s_recv.at[0])
    running = jnp.zeros((8, 128), f32)
    owned = jnp.zeros((8, 128), f32)
    for block in range(nctx - 1, -1, -1):
        s_recv[1, block] = running
        start = s_recv[0, block]
        running = running * block_own + start
        owned += start * (e_recv[1, block] + e_recv[0, block] * inverse_own)
    owned = owned * step_own
    lane_row = lax.broadcasted_iota(jnp.int32, (128, 128), 0)
    lane_column = lax.broadcasted_iota(jnp.int32, (128, 128), 1)
    chosen = (
        (lane_row // 64 == (lane_column % 16) // 8) & ((lane_row % 64) // 16 == lane_column // 16)
    ).astype(f32)
    summed = jnp.dot(owned, chosen, precision=highest, preferred_element_type=f32)
    right_row = lax.broadcasted_iota(jnp.int32, (8, 128), 0) == lanes % 8
    gradient = jnp.sum(jnp.where(right_row & lower, summed, 0.0), axis=0, keepdims=True)
    await_all(2, g_send, g_recv)
    for block in range(nctx):
        gradient += g_recv[block]
    p_send[...] = gradient

    def dp_copy(step, here):
        there = lax.rem(mine + step, ndp)
        return pltpu.make_async_remote_copy(
            src_ref=p_send,
            dst_ref=g_recv_dp.at[there if here else mine],
            send_sem=psend_sem.at[there],
            recv_sem=precv_sem.at[there if here else mine],
            device_id={"dp": there},
            device_id_type=MESH,
        )

    g_recv_dp = o_recv.at[1]
    for step in range(1, ndp):
        dp_copy(step, False).start()
    send_all(4, s_recv.at[1], p_recv.at[1])
    p_recv[1, me] = s_recv[1, me]
    g_recv_dp[mine] = gradient
    for step in range(1, ndp):
        dp_copy(step, True).wait_recv()
    gradient = g_recv_dp[0]
    for other in range(1, ndp):
        gradient += g_recv_dp[other]
    o_send[...] = gradient * scale
    send_all(5, o_send, o_recv.at[0], False)
    o_recv[0, me] = gradient * scale

    def finish(kind, back, number, table, local, target):
        await_all(kind, back, p_recv.at[number])
        carried = (unpack(p_recv.at[number]) + states[number] * coefs[1]) * coefs[0]
        for q in range(tiles):
            piece = slice(256 * q, 256 * q + 256)
            product = times((table[0, :, piece], table[1, :, piece]), split(on_blocks(carried, q)))
            target[0, :, piece] = (local[:, piece] + product).astype(bf16)

    finish(3, e_recv.at[1], 0, wf_ref, ylocal, y_ref)
    finish(4, s_recv.at[1], 1, wb_ref, zlocal, z_ref)
    await_all(5, o_send, o_recv.at[0], False)
    for pair in range(nctx // 2):
        first, second = o_recv[0, 2 * pair], o_recv[0, 2 * pair + 1]
        piece = slice(128 * pair, 128 * pair + 128)
        h_ref[0:1, 0:128] = jnp.where(lower_row, first, pltpu.roll(second, 64, 1))
        gskip_ref[:, piece] = jnp.where(lower_row, pltpu.roll(first, 64, 1), second)
        packs[0, pair, 0:1] = h_ref[0:1, 0:128]
    grad_row = jnp.concatenate([packs[0, pair, 0:1] for pair in range(nctx // 2)], axis=1) * weight_row
    gres_ref[...] = lax.dot_general(
        jnp.where(own_group, grad_row, 0.0), spread, (((1,), (1,)), ((), ())), precision=highest, preferred_element_type=f32
    )

    for load_kind in ((0, e_send, e_recv.at[0]), (1, s_send, s_recv.at[0]), (2, g_send, g_recv),
                      (3, e_recv.at[1], p_recv.at[0]), (4, s_recv.at[1], p_recv.at[1])):
        await_sent(*load_kind)
    await_sent(5, o_send, o_recv.at[0], False)
    for step in range(1, ndp):
        dp_copy(step, True).wait_send()


def transform(rows):
    frequency = np.pi * (2 * np.arange(rows // 2) + 1) / rows
    angle = frequency[:, None] * np.arange(rows)[None, :]
    forward = np.concatenate([np.cos(angle), -np.sin(angle)], axis=0)
    high = forward.astype(jnp.bfloat16)
    low = (forward - high.astype(np.float64)).astype(jnp.bfloat16)
    both = np.stack([high, low])
    back = (both.transpose(0, 2, 1).astype(np.float32) * (2.0 / rows)).astype(jnp.bfloat16)
    trig = np.zeros((rows // 2, 128), np.float32)
    trig[:, 0] = 2.0 * np.sin(frequency / 2.0) ** 2
    trig[:, 1] = np.sin(frequency)
    return jnp.asarray(both), jnp.asarray(back), jnp.asarray(trig)


def shards(nctx, ndp, inputs, cotangent, residues, decay_rates, skip_gain):
    _, rows, channels = inputs.shape
    groups, modes = residues.shape
    sizes = (nctx, ndp, rows, channels, groups, modes, 1.0 / math.sqrt(rows * nctx * ndp))
    forward, back, trig = transform(rows)
    anywhere = pl.BlockSpec(memory_space=pl.ANY)
    vmem = pl.BlockSpec(memory_space=pltpu.VMEM)
    wide = (1, rows, channels)
    outputs, grad_inputs, grad_residues, grad_skip = pl.pallas_call(
        functools.partial(kernel, sizes),
        out_shape=(
            jax.ShapeDtypeStruct(wide, bf16),
            jax.ShapeDtypeStruct(wide, bf16),
            jax.ShapeDtypeStruct((groups, modes), f32),
            jax.ShapeDtypeStruct((1, channels), f32),
        ),
        in_specs=[anywhere] * 8,
        out_specs=(vmem, vmem, vmem, vmem),
        scratch_shapes=[
            pltpu.VMEM((rows, channels), bf16),
            pltpu.VMEM((rows, channels), bf16),
            pltpu.VMEM((groups, modes), f32),
            pltpu.VMEM((groups, modes), f32),
            pltpu.VMEM((1, channels), f32),
            pltpu.VMEM((2, rows, rows), bf16),
            pltpu.VMEM((2, rows, rows), bf16),
            pltpu.VMEM((rows // 2, 128), f32),
            pltpu.VMEM((2, rows, channels), bf16),
            pltpu.VMEM((2, rows, channels), bf16),
            pltpu.VMEM((rows, 256), f32),
            pltpu.VMEM((rows, channels), f32),
            pltpu.VMEM((rows, channels), f32),
            pltpu.VMEM((2, modes, channels), f32),
            pltpu.VMEM((2, modes, channels), f32),
            pltpu.VMEM((3, nctx, 8, 128), f32),
            pltpu.VMEM((nctx, 8, 128), f32),
            pltpu.VMEM((2, nctx, 8, 128), f32),
            pltpu.VMEM((nctx, 8, 128), f32),
            pltpu.VMEM((2, nctx, 8, 128), f32),
            pltpu.VMEM((nctx, 1, 128), f32),
            pltpu.VMEM((nctx, 1, 128), f32),
            pltpu.VMEM((1, 128), f32),
            pltpu.VMEM((2, nctx, 8, 128), f32),
            pltpu.VMEM((1, 128), f32),
            pltpu.VMEM((2, nctx, 1, 128), f32),
            pltpu.SemaphoreType.DMA((8,)),
            pltpu.SemaphoreType.DMA((6, nctx)),
            pltpu.SemaphoreType.DMA((6, nctx)),
            pltpu.SemaphoreType.DMA((ndp,)),
            pltpu.SemaphoreType.DMA((ndp,)),
        ],
        compiler_params=pltpu.CompilerParams(collective_id=0, has_side_effects=True, vmem_limit_bytes=48 * 1024 * 1024),
        name="hyena",
    )(inputs, cotangent, residues, decay_rates, skip_gain.reshape(1, channels), forward, back, trig)
    return outputs, grad_inputs, grad_residues, grad_skip.reshape(channels)


def solution(mesh):
    placed = (P("dp", "ctx", "tp"), P("dp", "ctx", "tp"), P("tp", None), P("tp", None), P("tp"))
    return jax.shard_map(
        functools.partial(shards, mesh.shape["ctx"], mesh.shape["dp"]),
        mesh=mesh,
        in_specs=placed,
        out_specs=(P("dp", "ctx", "tp"), P("dp", "ctx", "tp"), P("tp", None), P("tp")),
        check_vma=False,
    )
```

time: 634 us -> 50.7 us (0.08)
  blocking collectives: 275 us -> 0 us
  matrix products: 163 us -> 0 us
  starting transfers between devices: 75.9 us -> 0 us
  waiting for transfers between devices: 74.7 us -> 0 us
  Pallas kernels: 0 us -> 41.3 us
  local copies, waits for them, and re-layouts: 34.5 us -> 8.44 us
    psum x1 -> x0, blocking collectives: 275 us -> none  [shards(): lax.psum(((local_grad + carried_grad) * scale, skip_local * scale), ('dp'...]
    dot_general x84 -> x0, matrix products: 163 us -> none  [the longest x16 43.6 us: local_block(): jnp.einsum('gmt,gts,gms->gm', down_piece, pairs, up_piece, precision=high...]
    ppermute x30 -> x0, starting transfers between devices: 75.9 us -> none  [passed_along(): return lax.ppermute(value, axis, pairs)]
    ppermute x30 -> x0, waiting for transfers between devices: 74.7 us -> none  [passed_along(): return lax.ppermute(value, axis, pairs)]
    pallas_call x0 -> x1, Pallas kernels: none -> 41.3 us  [shards(): pl.pallas_call(functools.partial(kernel, sizes), out_shape=(jax.ShapeDtyp...]
    squeeze x32 -> x0, local copies, waits for them, and re-layouts: 13.7 us -> none  [shards(): lax.map(local_block, (by_groups(coefficient), by_groups(decay_down), by_g...]
    broadcast_in_dim x32 -> x0, local copies, waits for them, and re-layouts: 6.89 us -> none  [the longest x15 4.06 us: relay_turn(): sent_x = incoming_x * passing + end_states]
  transfers between devices with their start and end apart: 30 -> 0, of which waited for: 30 -> 0; matrix products, arithmetic and copies ran while one was open for 0% -> 0% of each run, Pallas kernels for 0% -> 0%
where the time goes in v1:
time: 50.7 us; the launch traced here: 50.4 us
  Pallas kernels  41.3 us (81%)
  local copies, waits for them, and re-layouts  8.44 us (17%)
  between operations  0.67 us (1%)
    pallas_call x1, Pallas kernels, shards(): pl.pallas_call(functools.partial(kernel, sizes), out_shape=(jax.ShapeDtyp...  41.3 us
    unnamed x18, local copies, waits for them, and re-layouts  8.44 us

profile of v1, /device:TPU:24, one launch (start us, length us, event | category | flops | bytes accessed | tf_op | source)
XLA Modules:
  0.0 50.4 jit_solution(16758409031886785747)
XLA Ops:
  0.6 0.0 copy-start.4
  0.6 0.8 %copy.12.res_hbm = f32[64,16]{1,0:T(8,128)S(1)} copy(f32[64,16]{0,1:T(8,128)} %param.10) | data formatting | bytes 8192 | tf_op args[2]
  1.5 0.0 copy-start.5
  1.5 0.8 %copy.13.rate_hbm = f32[64,16]{1,0:T(8,128)S(1)} copy(f32[64,16]{0,1:T(8,128)} %param.11) | data formatting | bytes 8192 | tf_op args[3]
  2.2 0.0 copy-done.4
  2.3 0.0 copy-done.5
  2.3 0.0 copy-start
  2.3 1.0 %copy-done = bf16[1,256,1024]{2,1,0:T(8,128)(2,1)S(1)} copy-done((bf16[1,256,1024]{2,1,0:T(8,128)(2,1)S(1)}, bf16[1,256,1024]{2,1,0:T(8,128)(2,1)}, u32[]{:S(2)}) %copy-start) | copy-done | bytes 524312
  3.3 0.0 copy-start.1
  3.3 1.0 %copy-done.1 = bf16[1,256,1024]{2,1,0:T(8,128)(2,1)S(1)} copy-done((bf16[1,256,1024]{2,1,0:T(8,128)(2,1)S(1)}, bf16[1,256,1024]{2,1,0:T(8,128)(2,1)}, u32[]{:S(2)}) %copy-start.1) | copy-done | bytes 524312
  4.3 0.0 copy-start.2
  4.3 0.9 %copy-done.2 = bf16[2,256,256]{2,1,0:T(8,128)(2,1)S(1)} copy-done((bf16[2,256,256]{2,1,0:T(8,128)(2,1)S(1)}, bf16[2,256,256]{2,1,0:T(8,128)(2,1)}, u32[]{:S(2)}) %copy-start.2) | copy-done | bytes 262168
  5.3 0.0 copy-start.3
  5.3 0.9 %copy-done.3 = bf16[2,256,256]{2,1,0:T(8,128)(2,1)S(1)} copy-done((bf16[2,256,256]{2,1,0:T(8,128)(2,1)S(1)}, bf16[2,256,256]{2,1,0:T(8,128)(2,1)}, u32[]{:S(2)}) %copy-start.3) | copy-done | bytes 262168
  6.2 41.3 %hyena.1 = (bf16[1,256,1024]{2,1,0:T(8,128)(2,1)S(1)}, bf16[1,256,1024]{2,1,0:T(8,128)(2,1)S(1)}, f32[64,16]{1,0:T(8,128)S(1)}, f32[1,1024]{1,0:T(1,128)S(1)}) custom-call(bf16[1,256,1024]{2,1,0:T(8,128)(2,1)S(1)} %copy-done, bf16[1,256,1024]{2,1,0:T(8,128)(2,1)S(1)} %copy-done.1, f32[64,16]{1,0:T(8,128)S(1)} %copy.12.res_hbm, f32[64,16]{1,0:T(8,128)S(1)} %copy.13.rate_hbm, ...), custom_call_target="tpu_custom_call" | custom-call | tf_op jit(solution)/shard_map/hyena/pallas_call | solution.py:352
  47.5 0.7 %copy.14 = f32[64,16]{0,1:T(8,128)} copy(f32[64,16]{1,0:T(8,128)S(1)} %get-tuple-element.14) | data formatting | bytes 8192
  48.2 0.8 %copy.18 = bf16[1,256,1024]{2,1,0:T(8,128)(2,1)} copy(bf16[1,256,1024]{2,1,0:T(8,128)(2,1)S(1)} %get-tuple-element.20) | data formatting | bytes 1048576
  49.0 0.8 %copy.19 = bf16[1,256,1024]{2,1,0:T(8,128)(2,1)} copy(bf16[1,256,1024]{2,1,0:T(8,128)(2,1)S(1)} %get-tuple-element.21) | data formatting | bytes 1048576
  49.8 0.6 %copy.20 = f32[1024]{0:T(1024)} copy(f32[1024]{0:T(1024)S(1)} %bitcast.3) | data formatting | bytes 8192
Async XLA Ops:
  0.6 1.6 %copy-start.4 = (f32[128,128]{1,0:T(8,128)S(1)}, f32[128,128]{1,0:T(8,128)}, u32[]{:S(2)}) copy-start(f32[128,128]{1,0:T(8,128)} %constant.8.clone.trig_hbm) | copy-start | bytes 196612
  1.5 0.8 %copy-start.5 = (f32[1024]{0:T(1024)S(1)}, f32[1024]{0:T(1024)}, u32[]{:S(2)}) copy-start(f32[1024]{0:T(1024)} %param.12) | copy-start | bytes 12292
  2.3 1.0 %copy-start = (bf16[1,256,1024]{2,1,0:T(8,128)(2,1)S(1)}, bf16[1,256,1024]{2,1,0:T(8,128)(2,1)}, u32[]{:S(2)}) copy-start(bf16[1,256,1024]{2,1,0:T(8,128)(2,1)} %x_hbm.1) | copy-start | bytes 1572868
  3.3 1.0 %copy-start.1 = (bf16[1,256,1024]{2,1,0:T(8,128)(2,1)S(1)}, bf16[1,256,1024]{2,1,0:T(8,128)(2,1)}, u32[]{:S(2)}) copy-start(bf16[1,256,1024]{2,1,0:T(8,128)(2,1)} %d_hbm.1) | copy-start | bytes 1572868
  4.3 0.9 %copy-start.2 = (bf16[2,256,256]{2,1,0:T(8,128)(2,1)S(1)}, bf16[2,256,256]{2,1,0:T(8,128)(2,1)}, u32[]{:S(2)}) copy-start(bf16[2,256,256]{2,1,0:T(8,128)(2,1)} %constant.7.clone.inv_hbm) | copy-start | bytes 786436
  5.3 0.9 %copy-start.3 = (bf16[2,256,256]{2,1,0:T(8,128)(2,1)S(1)}, bf16[2,256,256]{2,1,0:T(8,128)(2,1)}, u32[]{:S(2)}) copy-start(bf16[2,256,256]{2,1,0:T(8,128)(2,1)} %constant.6.clone.fwd_hbm) | copy-start | bytes 786436

commit v2 on v1

v2 whole, which is shorter than its diff:
```python
import functools
import math

import jax
import jax.numpy as jnp
import numpy as np
from jax import lax
from jax.experimental import pallas as pl
from jax.experimental.pallas import tpu as pltpu
from jax.sharding import PartitionSpec as P

MESH = pl.DeviceIdType.MESH
highest = lax.Precision.HIGHEST
f32 = jnp.float32
bf16 = jnp.bfloat16
COMM = True
UNROLL = True


def split(value):
    high = value.astype(bf16)
    return high, (value - high.astype(f32)).astype(bf16)


def times(left, right):
    total = jnp.dot(left[0], right[0], preferred_element_type=f32)
    total += jnp.dot(left[0], right[1], preferred_element_type=f32)
    return total + jnp.dot(left[1], right[0], preferred_element_type=f32)


def times_row(left, right):
    return jnp.dot(left, right, precision=highest, preferred_element_type=f32)


def split_store(target, piece, value):
    high, low = split(value)
    target[0, :, piece] = high
    target[1, :, piece] = low


def same_block(shape):
    return lax.broadcasted_iota(jnp.int32, shape, 0) // 16 == lax.broadcasted_iota(jnp.int32, shape, 1) // 16


def on_blocks(piece):
    return jnp.where(same_block((256, 256)), jnp.concatenate([piece] * 16, axis=0), 0.0)


def off_blocks(array):
    return jnp.sum(jnp.where(same_block((256, 256)), array, 0.0).reshape(16, 16, 256), axis=0)


def kernel(sizes, x_hbm, d_hbm, res_hbm, rate_hbm, skip_hbm, fwd_hbm, inv_hbm, trig_hbm,
           y_ref, zlocal, wb_ref, carried_ref, gres_ref, gskip_ref,
           x_ref, d_ref, res_ref, rate_ref, skip_ref, fwd_ref, inv_ref, trig_ref,
           wf_ref, h_ref, ylocal, rate_row, states, coefs, packs, e_send, e_recv, s_send, s_recv,
           g_send, g_recv, p_send, p_recv, o_send, o_recv, load_sem, send_sem, recv_sem, psend_sem, precv_sem):
    nctx, ndp, rows, channels, groups, modes, scale = sizes
    half = rows // 2
    tiles = channels // 256
    me = lax.axis_index("ctx")
    mine = lax.axis_index("dp")

    barrier = pltpu.get_barrier_semaphore()

    def greet(step, carried):
        pl.semaphore_signal(barrier, inc=1, device_id={"ctx": lax.rem(me + step, nctx)}, device_id_type=MESH)
        return carried

    if COMM:
        lax.fori_loop(1, nctx, greet, 0)
        for step in range(1, ndp):
            pl.semaphore_signal(barrier, inc=1, device_id={"dp": lax.rem(mine + step, ndp)}, device_id_type=MESH)

    loads = [
        pltpu.make_async_copy(source, target, load_sem.at[number])
        for number, (source, target) in enumerate(
            [(rate_hbm, rate_ref), (res_hbm, res_ref), (x_hbm.at[0], x_ref), (d_hbm.at[0], d_ref), (trig_hbm, trig_ref),
             (fwd_hbm, fwd_ref), (inv_hbm, inv_ref), (skip_hbm, skip_ref)]
        )
    ]
    for load in loads:
        load.start()

    lanes = lax.broadcasted_iota(jnp.int32, (8, 128), 1)
    lower = lanes < 64
    lower_row = lax.broadcasted_iota(jnp.int32, (1, 128), 1) < 64
    positions = lax.broadcasted_iota(jnp.int32, (rows, 1), 0).astype(f32)
    own_group = (
        lax.broadcasted_iota(jnp.int32, (groups, channels), 1) // modes == lax.broadcasted_iota(jnp.int32, (groups, channels), 0)
    ).astype(f32)
    own_mode = (
        lax.broadcasted_iota(jnp.int32, (modes, channels), 1) % modes == lax.broadcasted_iota(jnp.int32, (modes, channels), 0)
    )

    def by_tiles(body):
        if UNROLL:
            for q in range(tiles):
                body(q, slice(256 * q, 256 * q + 256))
        else:
            def turn(q, carried):
                body(q, pl.ds(pl.multiple_of(q * 256, 256), 256))
                return carried

            lax.fori_loop(0, tiles, turn, 0)

    def pack(array, target):
        for pair in range(nctx // 2):
            low = array[0:8, 128 * pair : 128 * pair + 128]
            high = array[8:16, 128 * pair : 128 * pair + 128]
            target[2 * pair] = jnp.where(lower, low, pltpu.roll(high, 64, 1))
            target[2 * pair + 1] = jnp.where(lower, pltpu.roll(low, 64, 1), high)

    def unpack(source):
        lows, highs = [], []
        for pair in range(nctx // 2):
            first, second = source[2 * pair], source[2 * pair + 1]
            lows.append(jnp.where(lower, first, pltpu.roll(second, 64, 1)))
            highs.append(jnp.where(lower, pltpu.roll(first, 64, 1), second))
        return jnp.concatenate([jnp.concatenate(lows, axis=1), jnp.concatenate(highs, axis=1)], axis=0)

    def transposed_dot(left, right):
        return lax.dot_general(left, right, (((0,), (0,)), ((), ())), preferred_element_type=f32)

    loads[0].wait()
    rate_wide = times_row(rate_ref[...], own_group)
    rate_row[...] = jnp.sum(jnp.where(own_mode, rate_wide, 0.0), axis=0, keepdims=True)

    def end_states(q, piece):
        split_store(wb_ref, piece, jnp.exp(-rate_row[:, piece] * (rows - 1.0 - positions)))
        full = transposed_dot(wb_ref[0, :, piece], x_ref[:, piece]) + transposed_dot(wb_ref[1, :, piece], x_ref[:, piece])
        states[0, :, piece] = off_blocks(full)

    def start_states(q, piece):
        split_store(wf_ref, piece, jnp.exp(-rate_row[:, piece] * positions))
        full = transposed_dot(wf_ref[0, :, piece], d_ref[:, piece]) + transposed_dot(wf_ref[1, :, piece], d_ref[:, piece])
        states[1, :, piece] = off_blocks(full)

    loads[2].wait()
    by_tiles(end_states)
    pack(states[0], e_send)
    loads[3].wait()
    by_tiles(start_states)
    pack(states[1], s_send)

    def state_copy(there, kind, send, recv, slot_there):
        return pltpu.make_async_remote_copy(
            src_ref=send.at[there] if kind < 5 else send,
            dst_ref=recv.at[slot_there],
            send_sem=send_sem.at[kind, there],
            recv_sem=recv_sem.at[kind, slot_there],
            device_id={"ctx": there},
            device_id_type=MESH,
        )

    def over_peers(body):
        def turn(step, carried):
            body(lax.rem(me + step, nctx))
            return carried

        if COMM:
            lax.fori_loop(1, nctx, turn, 0)

    def send_all(kind, send, recv):
        def turn(count, carried):
            step = nctx // 2 + jnp.where(count % 2 == 1, -((count + 1) // 2), count // 2)
            state_copy(lax.rem(me + step, nctx), kind, send, recv, me).start()
            return carried

        if COMM:
            lax.fori_loop(0, nctx - 1, turn, 0)

    def await_all(kind, send, recv):
        over_peers(lambda origin: state_copy(origin, kind, send, recv, origin).wait_recv())

    def await_sent(kind, send, recv):
        over_peers(lambda origin: state_copy(origin, kind, send, recv, origin).wait_send())

    if COMM:
        pl.semaphore_wait(barrier, nctx - 1 + ndp - 1)
    send_all(0, e_send, e_recv.at[0])
    send_all(1, s_send, s_recv.at[0])
    e_recv[0, me] = e_send[me]
    s_recv[0, me] = s_send[me]

    loads[1].wait()
    coefs[0] = times_row(res_ref[...], own_group) * jnp.sqrt(1.0 - jnp.exp(-2.0 * rate_wide))
    step_wide = jnp.exp(-rate_wide)
    block_wide = jnp.exp(-rate_wide * float(rows))
    inverse_wide = 1.0 / (1.0 + block_wide)
    coefs[1] = coefs[0] * step_wide
    coefs[2] = inverse_wide
    pack(block_wide, packs.at[0])
    pack(inverse_wide, packs.at[1])
    pack(step_wide, packs.at[2])
    for load in loads[4:]:
        load.wait()

    def own_part(q, piece):
        step_piece = jnp.exp(-rate_row[:, piece])
        less_cos, sine = trig_ref[:, 0:1], trig_ref[:, 1:2]
        rest = 1.0 - step_piece
        near = step_piece * less_cos
        below = 1.0 / (rest * rest + 2.0 * near)
        h_ref[0:half] = (rest + near) * below
        h_ref[half:rows] = (-step_piece * sine) * below
        response = times(split(h_ref[...]), split(on_blocks(coefs[0, :, piece])))
        f_re, f_im = response[0:half], response[half:rows]
        x_piece, d_piece = x_ref[:, piece], d_ref[:, piece]
        x_hat = jnp.dot(fwd_ref[0], x_piece, preferred_element_type=f32) + jnp.dot(fwd_ref[1], x_piece, preferred_element_type=f32)
        d_hat = jnp.dot(fwd_ref[0], d_piece, preferred_element_type=f32) + jnp.dot(fwd_ref[1], d_piece, preferred_element_type=f32)
        x_re, x_im, d_re, d_im = x_hat[0:half], x_hat[half:rows], d_hat[0:half], d_hat[half:rows]
        skip = skip_ref[:, piece]
        x_wide, d_wide = x_piece.astype(f32), d_piece.astype(f32)
        y_hat = jnp.concatenate([f_re * x_re - f_im * x_im, f_re * x_im + f_im * x_re], axis=0)
        ylocal[:, piece] = times((inv_ref[0], inv_ref[1]), split(y_hat)) + skip * x_wide
        z_hat = jnp.concatenate([f_re * d_re + f_im * d_im, f_re * d_im - f_im * d_re], axis=0)
        zlocal[:, piece] = times((inv_ref[0], inv_ref[1]), split(z_hat)) + skip * d_wide
        cross = jnp.concatenate([d_re * x_re + d_im * x_im, d_im * x_re - d_re * x_im], axis=0)
        cross_high, cross_low = split(cross)
        ones = same_block((256, 256)).astype(bf16)
        grouped = jnp.dot(cross_high, ones, preferred_element_type=f32) + jnp.dot(cross_low, ones, preferred_element_type=f32)
        grad_piece = jnp.sum(grouped * h_ref[...], axis=0, keepdims=True) * (2.0 / rows)
        skip_piece = jnp.sum(x_wide * d_wide, axis=0, keepdims=True)
        for part in range(2):
            pair = 2 * q + part
            grad_row, skip_row = grad_piece[:, 128 * part : 128 * part + 128], skip_piece[:, 128 * part : 128 * part + 128]
            g_send[2 * pair] = jnp.where(lower_row, grad_row, pltpu.roll(skip_row, 64, 1))
            g_send[2 * pair + 1] = jnp.where(lower_row, pltpu.roll(grad_row, 64, 1), skip_row)

    by_tiles(own_part)
    send_all(2, g_send, g_recv)
    g_recv[me] = g_send[me]

    block_own, inverse_own, step_own = packs[0, me], packs[1, me], packs[2, me]
    await_all(0, e_send, e_recv.at[0])
    running = jnp.zeros((8, 128), f32)
    for block in range(nctx):
        e_recv[1, block] = running
        running = running * block_own + e_recv[0, block]
    send_all(3, e_recv.at[1], p_recv.at[0])
    p_recv[0, me] = e_recv[1, me]
    await_all(1, s_send, s_recv.at[0])
    running = jnp.zeros((8, 128), f32)
    owned = jnp.zeros((8, 128), f32)
    for block in range(nctx - 1, -1, -1):
        s_recv[1, block] = running
        start = s_recv[0, block]
        running = running * block_own + start
        owned += start * (e_recv[1, block] + e_recv[0, block] * inverse_own)
    owned = owned * step_own
    lane_row = lax.broadcasted_iota(jnp.int32, (128, 128), 0)
    lane_column = lax.broadcasted_iota(jnp.int32, (128, 128), 1)
    chosen = (
        (lane_row // 64 == (lane_column % 16) // 8) & ((lane_row % 64) // 16 == lane_column // 16)
    ).astype(f32)
    summed = times_row(owned, chosen)
    right_row = lax.broadcasted_iota(jnp.int32, (8, 128), 0) == lanes % 8
    gradient = jnp.sum(jnp.where(right_row & lower, summed, 0.0), axis=0, keepdims=True)
    await_all(2, g_send, g_recv)
    for block in range(nctx):
        gradient += g_recv[block]
    p_send[...] = gradient
    from_dp = o_recv.at[1]

    def dp_copy(step, here):
        there = lax.rem(mine + step, ndp)
        slot = there if here else mine
        return pltpu.make_async_remote_copy(
            src_ref=p_send,
            dst_ref=from_dp.at[slot],
            send_sem=psend_sem.at[there],
            recv_sem=precv_sem.at[slot],
            device_id={"dp": there},
            device_id_type=MESH,
        )

    if COMM:
        for step in range(1, ndp):
            dp_copy(step, False).start()
    send_all(4, s_recv.at[1], p_recv.at[1])
    p_recv[1, me] = s_recv[1, me]
    from_dp[mine] = gradient
    if COMM:
        for step in range(1, ndp):
            dp_copy(step, True).wait_recv()
    gradient = from_dp[0]
    for other in range(1, ndp):
        gradient += from_dp[other]
    o_send[...] = gradient * scale
    send_all(5, o_send, o_recv.at[0])
    o_recv[0, me] = gradient * scale

    await_all(3, e_recv.at[1], p_recv.at[0])
    carried_ref[...] = (unpack(p_recv.at[0]) + states[0] * coefs[2]) * coefs[1]

    def finish(q, piece):
        product = times((wf_ref[0, :, piece], wf_ref[1, :, piece]), split(on_blocks(carried_ref[:, piece])))
        y_ref[:, piece] = (ylocal[:, piece] + product).astype(bf16)

    by_tiles(finish)
    await_all(4, s_recv.at[1], p_recv.at[1])
    carried_ref[...] = (unpack(p_recv.at[1]) + states[1] * coefs[2]) * coefs[1]
    await_all(5, o_send, o_recv.at[0])
    final = []
    for pair in range(nctx // 2):
        first, second = o_recv[0, 2 * pair], o_recv[0, 2 * pair + 1]
        gskip_ref[:, 128 * pair : 128 * pair + 128] = jnp.where(lower_row, pltpu.roll(first, 64, 1), second)
        final.append(jnp.where(lower_row, first, pltpu.roll(second, 64, 1)))
    by_group = lax.dot_general(
        jnp.where(own_mode, jnp.concatenate(final, axis=1), 0.0), own_group, (((1,), (1,)), ((), ())), precision=highest,
        preferred_element_type=f32,
    )
    gres_ref[...] = by_group * jnp.sqrt(1.0 - jnp.exp(-2.0 * rate_ref[...]))

    for sent in ((0, e_send, e_recv.at[0]), (1, s_send, s_recv.at[0]), (2, g_send, g_recv),
                 (3, e_recv.at[1], p_recv.at[0]), (4, s_recv.at[1], p_recv.at[1]), (5, o_send, o_recv.at[0])):
        await_sent(*sent)
    if COMM:
        for step in range(1, ndp):
            dp_copy(step, True).wait_send()


def last_kernel(y_in, zlocal, wb_ref, carried_ref, gres_in, gskip_in, y_hbm, z_hbm, gres_hbm, gskip_hbm, z_ref, sem):
    tiles = zlocal.shape[1] // 256
    copies = [
        pltpu.make_async_copy(source, target, sem.at[number])
        for number, (source, target) in enumerate([(y_in, y_hbm.at[0]), (gres_in, gres_hbm), (gskip_in, gskip_hbm)])
    ]
    for copy in copies:
        copy.start()
    for q in range(tiles):
        piece = slice(256 * q, 256 * q + 256)
        product = times((wb_ref[0, :, piece], wb_ref[1, :, piece]), split(on_blocks(carried_ref[:, piece])))
        z_ref[:, piece] = (zlocal[:, piece] + product).astype(bf16)
        copy = pltpu.make_async_copy(z_ref.at[:, piece], z_hbm.at[0, :, piece], sem.at[3 + q])
        copy.start()
        copies.append(copy)
    for copy in copies:
        copy.wait()


def transform(rows):
    frequency = np.pi * (2 * np.arange(rows // 2) + 1) / rows
    angle = frequency[:, None] * np.arange(rows)[None, :]
    forward = np.concatenate([np.cos(angle), -np.sin(angle)], axis=0)
    high = forward.astype(jnp.bfloat16)
    low = (forward - high.astype(np.float64)).astype(jnp.bfloat16)
    both = np.stack([high, low])
    back = (both.transpose(0, 2, 1).astype(np.float32) * (2.0 / rows)).astype(jnp.bfloat16)
    trig = np.zeros((rows // 2, 128), np.float32)
    trig[:, 0] = 2.0 * np.sin(frequency / 2.0) ** 2
    trig[:, 1] = np.sin(frequency)
    return jnp.asarray(both), jnp.asarray(back), jnp.asarray(trig)


def shards(nctx, ndp, inputs, cotangent, residues, decay_rates, skip_gain):
    _, rows, channels = inputs.shape
    groups, modes = residues.shape
    sizes = (nctx, ndp, rows, channels, groups, modes, 1.0 / math.sqrt(rows * nctx * ndp))
    forward, back, trig = transform(rows)
    hbm = pl.BlockSpec(memory_space=pltpu.HBM)
    vmem = pl.BlockSpec(memory_space=pltpu.VMEM)
    wide = (1, rows, channels)
    parts = pl.pallas_call(
        functools.partial(kernel, sizes),
        out_shape=(
            jax.ShapeDtypeStruct((rows, channels), bf16),
            jax.ShapeDtypeStruct((rows, channels), f32),
            jax.ShapeDtypeStruct((2, rows, channels), bf16),
            jax.ShapeDtypeStruct((modes, channels), f32),
            jax.ShapeDtypeStruct((modes, groups), f32),
            jax.ShapeDtypeStruct((1, channels), f32),
        ),
        in_specs=[hbm] * 8,
        out_specs=(vmem,) * 6,
        scratch_shapes=[
            pltpu.VMEM((rows, channels), bf16),
            pltpu.VMEM((rows, channels), bf16),
            pltpu.VMEM((modes, groups), f32),
            pltpu.VMEM((modes, groups), f32),
            pltpu.VMEM((1, channels), f32),
            pltpu.VMEM((2, rows, rows), bf16),
            pltpu.VMEM((2, rows, rows), bf16),
            pltpu.VMEM((rows // 2, 128), f32),
            pltpu.VMEM((2, rows, channels), bf16),
            pltpu.VMEM((rows, 256), f32),
            pltpu.VMEM((rows, channels), f32),
            pltpu.VMEM((1, channels), f32),
            pltpu.VMEM((2, modes, channels), f32),
            pltpu.VMEM((3, modes, channels), f32),
            pltpu.VMEM((3, nctx, 8, 128), f32),
            pltpu.VMEM((nctx, 8, 128), f32),
            pltpu.VMEM((2, nctx, 8, 128), f32),
            pltpu.VMEM((nctx, 8, 128), f32),
            pltpu.VMEM((2, nctx, 8, 128), f32),
            pltpu.VMEM((nctx, 1, 128), f32),
            pltpu.VMEM((nctx, 1, 128), f32),
            pltpu.VMEM((1, 128), f32),
            pltpu.VMEM((2, nctx, 8, 128), f32),
            pltpu.VMEM((1, 128), f32),
            pltpu.VMEM((2, nctx, 1, 128), f32),
            pltpu.SemaphoreType.DMA((8,)),
            pltpu.SemaphoreType.DMA((6, nctx)),
            pltpu.SemaphoreType.DMA((6, nctx)),
            pltpu.SemaphoreType.DMA((ndp,)),
            pltpu.SemaphoreType.DMA((ndp,)),
        ],
        compiler_params=pltpu.CompilerParams(collective_id=0, has_side_effects=True, vmem_limit_bytes=32 * 1024 * 1024),
        name="hyena",
    )(*[pltpu.with_memory_space_constraint(a, pltpu.HBM) for a in (inputs, cotangent, residues.T, decay_rates.T, skip_gain.reshape(1, channels), forward, back, trig)])
    outputs, grad_inputs, grad_residues, grad_skip = pl.pallas_call(
        last_kernel,
        out_shape=(
            jax.ShapeDtypeStruct(wide, bf16),
            jax.ShapeDtypeStruct(wide, bf16),
            jax.ShapeDtypeStruct((modes, groups), f32),
            jax.ShapeDtypeStruct((1, channels), f32),
        ),
        in_specs=[vmem] * 6,
        out_specs=(hbm,) * 4,
        scratch_shapes=[pltpu.VMEM((rows, channels), bf16), pltpu.SemaphoreType.DMA((3 + channels // 256,))],
        compiler_params=pltpu.CompilerParams(vmem_limit_bytes=32 * 1024 * 1024),
        name="last",
    )(*parts)
    return outputs, grad_inputs, grad_residues.T, grad_skip.reshape(channels)


def solution(mesh):
    placed = (P("dp", "ctx", "tp"), P("dp", "ctx", "tp"), P("tp", None), P("tp", None), P("tp"))
    return jax.shard_map(
        functools.partial(shards, mesh.shape["ctx"], mesh.shape["dp"]),
        mesh=mesh,
        in_specs=placed,
        out_specs=(P("dp", "ctx", "tp"), P("dp", "ctx", "tp"), P("tp", None), P("tp")),
        check_vma=False,
    )
```

time: 50.7 us -> 43.2 us (0.85)
  local copies, waits for them, and re-layouts: 8.44 us -> 0 us
  Pallas kernels: 41.3 us -> 42.4 us
    unnamed x18 -> x0, local copies, waits for them, and re-layouts: 8.44 us -> none
    pallas_call x0 -> x1, Pallas kernels: none -> 1.41 us  [shards(): pl.pallas_call(last_kernel, out_shape=(jax.ShapeDtypeStruct(wide, bf16),...]
where the time goes in v2:
time: 43.2 us; the launch traced here: 43.1 us
  Pallas kernels  42.4 us (98%)
  between operations  0.64 us (1%)
    pallas_call x1, Pallas kernels, shards(): pl.pallas_call(functools.partial(kernel, sizes), out_shape=(jax.ShapeDtyp...  41 us
    pallas_call x1, Pallas kernels, shards(): pl.pallas_call(last_kernel, out_shape=(jax.ShapeDtypeStruct(wide, bf16),...  1.41 us

profile of v2, /device:TPU:24, one launch (start us, length us, event | category | flops | bytes accessed | tf_op | source)
XLA Modules:
  0.0 43.1 jit_solution(4116861146049266302)
XLA Ops:
  0.6 41.0 %hyena.1 = (bf16[256,1024]{1,0:T(8,128)(2,1)S(1)}, f32[256,1024]{1,0:T(8,128)S(1)}, bf16[2,256,1024]{2,1,0:T(8,128)(2,1)S(1)}, f32[16,1024]{1,0:T(8,128)S(1)}, f...) custom-call(bf16[1,256,1024]{2,1,0:T(8,128)(2,1)} %x_hbm.1, bf16[1,256,1024]{2,1,0:T(8,128)(2,1)} %d_hbm.1, f32[16,64]{1,0:T(8,128)} %bitcast.5, ...), custom_call_target="tpu_custom_call" | custom-call | tf_op jit(solution)/shard_map/hyena/pallas_call | solution.py:365
  41.7 1.4 %last.1 = (bf16[1,256,1024]{2,1,0:T(8,128)(2,1)}, bf16[1,256,1024]{2,1,0:T(8,128)(2,1)}, f32[16,64]{1,0:T(8,128)}, f32[1,1024]{1,0:T(1,128)}) custom-call(bf16[256,1024]{1,0:T(8,128)(2,1)S(1)} %get-tuple-element.14.y_in, f32[256,1024]{1,0:T(8,128)S(1)} %get-tuple-element.15.zlocal, bf16[2,256,1024]{2,1,0:T(8,128)(2,1)S(1)} %get-tuple-element.16.wb_ref, ...), custom_call_target="tpu_custom_call" | custom-call | tf_op jit(solution)/shard_map/last/pallas_call | solution.py:412

commit v3 on v2

--- a/solution.py
+++ b/solution.py
@@ -51,9 +51,9 @@
 
 
 def kernel(sizes, x_hbm, d_hbm, res_hbm, rate_hbm, skip_hbm, fwd_hbm, inv_hbm, trig_hbm,
-           y_ref, zlocal, wb_ref, carried_ref, gres_ref, gskip_ref,
+           y_ref, zlocal, wb_ref, carried_ref, final_ref,
            x_ref, d_ref, res_ref, rate_ref, skip_ref, fwd_ref, inv_ref, trig_ref,
-           wf_ref, h_ref, ylocal, rate_row, states, coefs, packs, e_send, e_recv, s_send, s_recv,
+           wf_ref, h_ref, x_hat, d_hat, ylocal, rate_row, states, coefs, packs, e_send, e_recv, s_send, s_recv,
            g_send, g_recv, p_send, p_recv, o_send, o_recv, load_sem, send_sem, recv_sem, psend_sem, precv_sem):
     nctx, ndp, rows, channels, groups, modes, scale = sizes
     half = rows // 2
@@ -176,12 +176,45 @@
     def await_sent(kind, send, recv):
         over_peers(lambda origin: state_copy(origin, kind, send, recv, origin).wait_send())
 
+    for load in loads[4:]:
+        load.wait()
+
+    def spectra(q, piece):
+        step_piece = jnp.exp(-rate_row[:, piece])
+        less_cos, sine = trig_ref[:, 0:1], trig_ref[:, 1:2]
+        rest = 1.0 - step_piece
+        near = step_piece * less_cos
+        below = 1.0 / (rest * rest + 2.0 * near)
+        h_ref[0:half, piece] = (rest + near) * below
+        h_ref[half:rows, piece] = (-step_piece * sine) * below
+        x_piece, d_piece = x_ref[:, piece], d_ref[:, piece]
+        x_new = jnp.dot(fwd_ref[0], x_piece, preferred_element_type=f32) + jnp.dot(fwd_ref[1], x_piece, preferred_element_type=f32)
+        d_new = jnp.dot(fwd_ref[0], d_piece, preferred_element_type=f32) + jnp.dot(fwd_ref[1], d_piece, preferred_element_type=f32)
+        x_hat[:, piece] = x_new
+        d_hat[:, piece] = d_new
+        x_re, x_im, d_re, d_im = x_new[0:half], x_new[half:rows], d_new[0:half], d_new[half:rows]
+        cross = jnp.concatenate([d_re * x_re + d_im * x_im, d_im * x_re - d_re * x_im], axis=0)
+        cross_high, cross_low = split(cross)
+        ones = same_block((256, 256)).astype(bf16)
+        grouped = jnp.dot(cross_high, ones, preferred_element_type=f32) + jnp.dot(cross_low, ones, preferred_element_type=f32)
+        grad_piece = jnp.sum(grouped * h_ref[:, piece], axis=0, keepdims=True) * (2.0 / rows)
+        skip_piece = jnp.sum(x_piece.astype(f32) * d_piece.astype(f32), axis=0, keepdims=True)
+        for part in range(2):
+            pair = 2 * q + part
+            grad_row, skip_row = grad_piece[:, 128 * part : 128 * part + 128], skip_piece[:, 128 * part : 128 * part + 128]
+            g_send[2 * pair] = jnp.where(lower_row, grad_row, pltpu.roll(skip_row, 64, 1))
+            g_send[2 * pair + 1] = jnp.where(lower_row, pltpu.roll(grad_row, 64, 1), skip_row)
+
+    by_tiles(spectra)
+
     if COMM:
         pl.semaphore_wait(barrier, nctx - 1 + ndp - 1)
     send_all(0, e_send, e_recv.at[0])
+    send_all(2, g_send, g_recv)
     send_all(1, s_send, s_recv.at[0])
     e_recv[0, me] = e_send[me]
     s_recv[0, me] = s_send[me]
+    g_recv[me] = g_send[me]
 
     loads[1].wait()
     coefs[0] = times_row(res_ref[...], own_group) * jnp.sqrt(1.0 - jnp.exp(-2.0 * rate_wide))
@@ -193,44 +226,18 @@
     pack(block_wide, packs.at[0])
     pack(inverse_wide, packs.at[1])
     pack(step_wide, packs.at[2])
-    for load in loads[4:]:
-        load.wait()
 
     def own_part(q, piece):
-        step_piece = jnp.exp(-rate_row[:, piece])
-        less_cos, sine = trig_ref[:, 0:1], trig_ref[:, 1:2]
-        rest = 1.0 - step_piece
-        near = step_piece * less_cos
-        below = 1.0 / (rest * rest + 2.0 * near)
-        h_ref[0:half] = (rest + near) * below
-        h_ref[half:rows] = (-step_piece * sine) * below
-        response = times(split(h_ref[...]), split(on_blocks(coefs[0, :, piece])))
+        response = times(split(h_ref[:, piece]), split(on_blocks(coefs[0, :, piece])))
         f_re, f_im = response[0:half], response[half:rows]
-        x_piece, d_piece = x_ref[:, piece], d_ref[:, piece]
-        x_hat = jnp.dot(fwd_ref[0], x_piece, preferred_element_type=f32) + jnp.dot(fwd_ref[1], x_piece, preferred_element_type=f32)
-        d_hat = jnp.dot(fwd_ref[0], d_piece, preferred_element_type=f32) + jnp.dot(fwd_ref[1], d_piece, preferred_element_type=f32)
-        x_re, x_im, d_re, d_im = x_hat[0:half], x_hat[half:rows], d_hat[0:half], d_hat[half:rows]
+        x_re, x_im, d_re, d_im = x_hat[0:half, piece], x_hat[half:rows, piece], d_hat[0:half, piece], d_hat[half:rows, piece]
         skip = skip_ref[:, piece]
-        x_wide, d_wide = x_piece.astype(f32), d_piece.astype(f32)
         y_hat = jnp.concatenate([f_re * x_re - f_im * x_im, f_re * x_im + f_im * x_re], axis=0)
-        ylocal[:, piece] = times((inv_ref[0], inv_ref[1]), split(y_hat)) + skip * x_wide
+        ylocal[:, piece] = times((inv_ref[0], inv_ref[1]), split(y_hat)) + skip * x_ref[:, piece].astype(f32)
         z_hat = jnp.concatenate([f_re * d_re + f_im * d_im, f_re * d_im - f_im * d_re], axis=0)
-        zlocal[:, piece] = times((inv_ref[0], inv_ref[1]), split(z_hat)) + skip * d_wide
-        cross = jnp.concatenate([d_re * x_re + d_im * x_im, d_im * x_re - d_re * x_im], axis=0)
-        cross_high, cross_low = split(cross)
-        ones = same_block((256, 256)).astype(bf16)
-        grouped = jnp.dot(cross_high, ones, preferred_element_type=f32) + jnp.dot(cross_low, ones, preferred_element_type=f32)
-        grad_piece = jnp.sum(grouped * h_ref[...], axis=0, keepdims=True) * (2.0 / rows)
-        skip_piece = jnp.sum(x_wide * d_wide, axis=0, keepdims=True)
-        for part in range(2):
-            pair = 2 * q + part
-            grad_row, skip_row = grad_piece[:, 128 * part : 128 * part + 128], skip_piece[:, 128 * part : 128 * part + 128]
-            g_send[2 * pair] = jnp.where(lower_row, grad_row, pltpu.roll(skip_row, 64, 1))
-            g_send[2 * pair + 1] = jnp.where(lower_row, pltpu.roll(grad_row, 64, 1), skip_row)
+        zlocal[:, piece] = times((inv_ref[0], inv_ref[1]), split(z_hat)) + skip * d_ref[:, piece].astype(f32)
 
     by_tiles(own_part)
-    send_all(2, g_send, g_recv)
-    g_recv[me] = g_send[me]
 
     block_own, inverse_own, step_own = packs[0, me], packs[1, me], packs[2, me]
     await_all(0, e_send, e_recv.at[0])
@@ -240,6 +247,10 @@
         running = running * block_own + e_recv[0, block]
     send_all(3, e_recv.at[1], p_recv.at[0])
     p_recv[0, me] = e_recv[1, me]
+    await_all(2, g_send, g_recv)
+    gradient = g_recv[0]
+    for block in range(1, nctx):
+        gradient += g_recv[block]
     await_all(1, s_send, s_recv.at[0])
     running = jnp.zeros((8, 128), f32)
     owned = jnp.zeros((8, 128), f32)
@@ -248,18 +259,15 @@
         start = s_recv[0, block]
         running = running * block_own + start
         owned += start * (e_recv[1, block] + e_recv[0, block] * inverse_own)
-    owned = owned * step_own
+    high, low = split(owned * step_own)
     lane_row = lax.broadcasted_iota(jnp.int32, (128, 128), 0)
     lane_column = lax.broadcasted_iota(jnp.int32, (128, 128), 1)
     chosen = (
         (lane_row // 64 == (lane_column % 16) // 8) & ((lane_row % 64) // 16 == lane_column // 16)
-    ).astype(f32)
-    summed = times_row(owned, chosen)
+    ).astype(bf16)
+    summed = jnp.dot(high, chosen, preferred_element_type=f32) + jnp.dot(low, chosen, preferred_element_type=f32)
     right_row = lax.broadcasted_iota(jnp.int32, (8, 128), 0) == lanes % 8
-    gradient = jnp.sum(jnp.where(right_row & lower, summed, 0.0), axis=0, keepdims=True)
-    await_all(2, g_send, g_recv)
-    for block in range(nctx):
-        gradient += g_recv[block]
+    gradient += jnp.sum(jnp.where(right_row & lower, summed, 0.0), axis=0, keepdims=True)
     p_send[...] = gradient
     from_dp = o_recv.at[1]
 
@@ -302,16 +310,7 @@
     await_all(4, s_recv.at[1], p_recv.at[1])
     carried_ref[...] = (unpack(p_recv.at[1]) + states[1] * coefs[2]) * coefs[1]
     await_all(5, o_send, o_recv.at[0])
-    final = []
-    for pair in range(nctx // 2):
-        first, second = o_recv[0, 2 * pair], o_recv[0, 2 * pair + 1]
-        gskip_ref[:, 128 * pair : 128 * pair + 128] = jnp.where(lower_row, pltpu.roll(first, 64, 1), second)
-        final.append(jnp.where(lower_row, first, pltpu.roll(second, 64, 1)))
-    by_group = lax.dot_general(
-        jnp.where(own_mode, jnp.concatenate(final, axis=1), 0.0), own_group, (((1,), (1,)), ((), ())), precision=highest,
-        preferred_element_type=f32,
-    )
-    gres_ref[...] = by_group * jnp.sqrt(1.0 - jnp.exp(-2.0 * rate_ref[...]))
+    final_ref[...] = o_recv[0]
 
     for sent in ((0, e_send, e_recv.at[0]), (1, s_send, s_recv.at[0]), (2, g_send, g_recv),
                  (3, e_recv.at[1], p_recv.at[0]), (4, s_recv.at[1], p_recv.at[1]), (5, o_send, o_recv.at[0])):
@@ -321,21 +320,41 @@
             dp_copy(step, True).wait_send()
 
 
-def last_kernel(y_in, zlocal, wb_ref, carried_ref, gres_in, gskip_in, y_hbm, z_hbm, gres_hbm, gskip_hbm, z_ref, sem):
-    tiles = zlocal.shape[1] // 256
-    copies = [
-        pltpu.make_async_copy(source, target, sem.at[number])
-        for number, (source, target) in enumerate([(y_in, y_hbm.at[0]), (gres_in, gres_hbm), (gskip_in, gskip_hbm)])
-    ]
-    for copy in copies:
-        copy.start()
-    for q in range(tiles):
+def last_kernel(y_in, zlocal, wb_ref, carried_ref, final_ref, rate_ref, y_hbm, z_hbm, gres_hbm, gskip_hbm,
+                z_ref, gres_ref, gskip_ref, sem):
+    channels = zlocal.shape[1]
+    modes, groups = rate_ref.shape
+    copies = []
+
+    def send(source, target):
+        copies.append(pltpu.make_async_copy(source, target, sem.at[len(copies)]))
+        copies[-1].start()
+
+    send(y_in, y_hbm.at[0])
+    for q in range(channels // 256):
         piece = slice(256 * q, 256 * q + 256)
         product = times((wb_ref[0, :, piece], wb_ref[1, :, piece]), split(on_blocks(carried_ref[:, piece])))
         z_ref[:, piece] = (zlocal[:, piece] + product).astype(bf16)
-        copy = pltpu.make_async_copy(z_ref.at[:, piece], z_hbm.at[0, :, piece], sem.at[3 + q])
-        copy.start()
-        copies.append(copy)
+        send(z_ref.at[:, piece], z_hbm.at[0, :, piece])
+    lower_row = lax.broadcasted_iota(jnp.int32, (1, 128), 1) < 64
+    final = []
+    for pair in range(channels // 128):
+        first, second = final_ref[2 * pair], final_ref[2 * pair + 1]
+        gskip_ref[:, 128 * pair : 128 * pair + 128] = jnp.where(lower_row, pltpu.roll(first, 64, 1), second)
+        final.append(jnp.where(lower_row, first, pltpu.roll(second, 64, 1)))
+    send(gskip_ref, gskip_hbm)
+    own_group = (
+        lax.broadcasted_iota(jnp.int32, (groups, channels), 1) // modes == lax.broadcasted_iota(jnp.int32, (groups, channels), 0)
+    ).astype(bf16)
+    own_mode = (
+        lax.broadcasted_iota(jnp.int32, (modes, channels), 1) % modes == lax.broadcasted_iota(jnp.int32, (modes, channels), 0)
+    )
+    high, low = split(jnp.where(own_mode, jnp.concatenate(final, axis=1), 0.0))
+    over_lanes = (((1,), (1,)), ((), ()))
+    by_group = lax.dot_general(high, own_group, over_lanes, preferred_element_type=f32)
+    by_group += lax.dot_general(low, own_group, over_lanes, preferred_element_type=f32)
+    gres_ref[...] = by_group * jnp.sqrt(1.0 - jnp.exp(-2.0 * rate_ref[...]))
+    send(gres_ref, gres_hbm)
     for copy in copies:
         copy.wait()
 
@@ -369,11 +388,10 @@
             jax.ShapeDtypeStruct((rows, channels), f32),
             jax.ShapeDtypeStruct((2, rows, channels), bf16),
             jax.ShapeDtypeStruct((modes, channels), f32),
-            jax.ShapeDtypeStruct((modes, groups), f32),
-            jax.ShapeDtypeStruct((1, channels), f32),
+            jax.ShapeDtypeStruct((nctx, 1, 128), f32),
         ),
         in_specs=[hbm] * 8,
-        out_specs=(vmem,) * 6,
+        out_specs=(vmem,) * 5,
         scratch_shapes=[
             pltpu.VMEM((rows, channels), bf16),
             pltpu.VMEM((rows, channels), bf16),
@@ -384,7 +402,9 @@
             pltpu.VMEM((2, rows, rows), bf16),
             pltpu.VMEM((rows // 2, 128), f32),
             pltpu.VMEM((2, rows, channels), bf16),
-            pltpu.VMEM((rows, 256), f32),
+            pltpu.VMEM((rows, channels), f32),
+            pltpu.VMEM((rows, channels), f32),
+            pltpu.VMEM((rows, channels), f32),
             pltpu.VMEM((rows, channels), f32),
             pltpu.VMEM((1, channels), f32),
             pltpu.VMEM((2, modes, channels), f32),
@@ -419,10 +439,15 @@
         ),
         in_specs=[vmem] * 6,
         out_specs=(hbm,) * 4,
-        scratch_shapes=[pltpu.VMEM((rows, channels), bf16), pltpu.SemaphoreType.DMA((3 + channels // 256,))],
+        scratch_shapes=[
+            pltpu.VMEM((rows, channels), bf16),
+            pltpu.VMEM((modes, groups), f32),
+            pltpu.VMEM((1, channels), f32),
+            pltpu.SemaphoreType.DMA((3 + channels // 256,)),
+        ],
         compiler_params=pltpu.CompilerParams(vmem_limit_bytes=32 * 1024 * 1024),
         name="last",
-    )(*parts)
+    )(*parts, decay_rates.T)
     return outputs, grad_inputs, grad_residues.T, grad_skip.reshape(channels)
 
 

time: 43.2 us -> 42.6 us (0.986)
  Pallas kernels: 42.4 us -> 41.1 us
  local copies, waits for them, and re-layouts: 0 us -> 0.69 us
    pallas_call x1, Pallas kernels: 41 us -> 39.6 us  [shards(): pl.pallas_call(functools.partial(kernel, sizes), out_shape=(jax.ShapeDtyp...]
    unnamed x0 -> x2, local copies, waits for them, and re-layouts: none -> 0.69 us
where the time goes in v3:
time: 42.6 us; the launch traced here: 42.4 us
  Pallas kernels  41.1 us (96%)
  local copies, waits for them, and re-layouts  0.69 us (2%)
  between operations  0.65 us (2%)
    pallas_call x1, Pallas kernels, shards(): pl.pallas_call(functools.partial(kernel, sizes), out_shape=(jax.ShapeDtyp...  39.6 us
    pallas_call x1, Pallas kernels, shards(): pl.pallas_call(last_kernel, out_shape=(jax.ShapeDtypeStruct(wide, bf16),...  1.44 us

profile of v3, /device:TPU:24, one launch (start us, length us, event | category | flops | bytes accessed | tf_op | source)
XLA Modules:
  0.0 42.4 jit_solution(1530247953516377398)
XLA Ops:
  0.6 39.6 %hyena.1 = (bf16[256,1024]{1,0:T(8,128)(2,1)S(1)}, f32[256,1024]{1,0:T(8,128)S(1)}, bf16[2,256,1024]{2,1,0:T(8,128)(2,1)S(1)}, f32[16,1024]{1,0:T(8,128)S(1)}, f32[16,1,128]{2,1,0:T(1,128)S(1)}) custom-call(bf16[1,256,1024]{2,1,0:T(8,128)(2,1)} %x_hbm.1, bf16[1,256,1024]{2,1,0:T(8,128)(2,1)} %d_hbm.1, f32[16,64]{1,0:T(8,128)} %bitcast.7, f32[16,64]{1,0:T(8,128)} %bitcast.5, ...), custom_call_target="tpu_custom_call" | custom-call | tf_op jit(solution)/shard_map/hyena/pallas_call | solution.py:384
  40.3 0.0 copy-start
  40.3 0.7 %copy-done = f32[64,16]{0,1:T(8,128)S(1)} copy-done((f32[64,16]{0,1:T(8,128)S(1)}, f32[64,16]{0,1:T(8,128)}, u32[]{:S(2)}) %copy-start) | copy-done | bytes 4120
  41.0 1.4 %last.1 = (bf16[1,256,1024]{2,1,0:T(8,128)(2,1)}, bf16[1,256,1024]{2,1,0:T(8,128)(2,1)}, f32[16,64]{1,0:T(8,128)}, f32[1,1024]{1,0:T(1,128)}) custom-call(bf16[256,1024]{1,0:T(8,128)(2,1)S(1)} %get-tuple-element.13.y_in, f32[256,1024]{1,0:T(8,128)S(1)} %get-tuple-element.14.zlocal, bf16[2,256,1024]{2,1,0:T(8,128)(2,1)S(1)} %get-tuple-element.15.wb_ref, ...), custom_call_target="tpu_custom_call" | custom-call | tf_op jit(solution)/shard_map/last/pallas_call | solution.py:432
Async XLA Ops:
  40.3 0.7 %copy-start = (f32[64,16]{0,1:T(8,128)S(1)}, f32[64,16]{0,1:T(8,128)}, u32[]{:S(2)}) copy-start(f32[64,16]{0,1:T(8,128)} %param.11) | copy-start | bytes 12292

commit v4 on v3

--- a/solution.py
+++ b/solution.py
@@ -54,7 +54,7 @@
            y_ref, zlocal, wb_ref, carried_ref, final_ref,
            x_ref, d_ref, res_ref, rate_ref, skip_ref, fwd_ref, inv_ref, trig_ref,
            wf_ref, h_ref, x_hat, d_hat, ylocal, rate_row, states, coefs, packs, e_send, e_recv, s_send, s_recv,
-           g_send, g_recv, p_send, p_recv, o_send, o_recv, load_sem, send_sem, recv_sem, psend_sem, precv_sem):
+           g_send, g_recv, p_recv, o_send, o_recv, load_sem, send_sem, recv_sem, osend_sem, orecv_sem, ring_sem):
     nctx, ndp, rows, channels, groups, modes, scale = sizes
     half = rows // 2
     tiles = channels // 256
@@ -145,7 +145,7 @@
 
     def state_copy(there, kind, send, recv, slot_there):
         return pltpu.make_async_remote_copy(
-            src_ref=send.at[there] if kind < 5 else send,
+            src_ref=send.at[there],
             dst_ref=recv.at[slot_there],
             send_sem=send_sem.at[kind, there],
             recv_sem=recv_sem.at[kind, slot_there],
@@ -209,6 +209,8 @@
 
     if COMM:
         pl.semaphore_wait(barrier, nctx - 1 + ndp - 1)
+        for step in range(1, ndp):
+            pl.semaphore_signal(ring_sem, inc=1, device_id={"dp": lax.rem(mine + step, ndp)}, device_id_type=MESH)
     send_all(0, e_send, e_recv.at[0])
     send_all(2, g_send, g_recv)
     send_all(1, s_send, s_recv.at[0])
@@ -259,6 +261,8 @@
         start = s_recv[0, block]
         running = running * block_own + start
         owned += start * (e_recv[1, block] + e_recv[0, block] * inverse_own)
+    send_all(4, s_recv.at[1], p_recv.at[1])
+    p_recv[1, me] = s_recv[1, me]
     high, low = split(owned * step_own)
     lane_row = lax.broadcasted_iota(jnp.int32, (128, 128), 0)
     lane_column = lax.broadcasted_iota(jnp.int32, (128, 128), 1)
@@ -268,36 +272,34 @@
     summed = jnp.dot(high, chosen, preferred_element_type=f32) + jnp.dot(low, chosen, preferred_element_type=f32)
     right_row = lax.broadcasted_iota(jnp.int32, (8, 128), 0) == lanes % 8
     gradient += jnp.sum(jnp.where(right_row & lower, summed, 0.0), axis=0, keepdims=True)
-    p_send[...] = gradient
-    from_dp = o_recv.at[1]
-
-    def dp_copy(step, here):
-        there = lax.rem(mine + step, ndp)
-        slot = there if here else mine
+    o_send[...] = gradient * scale
+    o_recv[mine, me] = gradient * scale
+
+    def gradient_copy(part, there, slot_part, slot):
         return pltpu.make_async_remote_copy(
-            src_ref=p_send,
-            dst_ref=from_dp.at[slot],
-            send_sem=psend_sem.at[there],
-            recv_sem=precv_sem.at[slot],
-            device_id={"dp": there},
+            src_ref=o_send,
+            dst_ref=o_recv.at[slot_part, slot],
+            send_sem=osend_sem.at[part, there],
+            recv_sem=orecv_sem.at[slot_part, slot],
+            device_id={"dp": part, "ctx": there},
             device_id_type=MESH,
         )
 
+    def over_parts(body):
+        for offset in range(ndp):
+            part = lax.rem(mine + offset, ndp)
+
+            def turn(count, carried):
+                step = nctx // 2 + jnp.where(count % 2 == 1, -((count + 1) // 2), count // 2)
+                body(part, lax.rem(me + step, nctx))
+                return carried
+
+            if COMM:
+                lax.fori_loop(0, nctx - 1 if offset == 0 else nctx, turn, 0)
+
     if COMM:
-        for step in range(1, ndp):
-            dp_copy(step, False).start()
-    send_all(4, s_recv.at[1], p_recv.at[1])
-    p_recv[1, me] = s_recv[1, me]
-    from_dp[mine] = gradient
-    if COMM:
-        for step in range(1, ndp):
-            dp_copy(step, True).wait_recv()
-    gradient = from_dp[0]
-    for other in range(1, ndp):
-        gradient += from_dp[other]
-    o_send[...] = gradient * scale
-    send_all(5, o_send, o_recv.at[0])
-    o_recv[0, me] = gradient * scale
+        pl.semaphore_wait(ring_sem, ndp - 1)
+    over_parts(lambda part, there: gradient_copy(part, there, mine, me).start())
 
     await_all(3, e_recv.at[1], p_recv.at[0])
     carried_ref[...] = (unpack(p_recv.at[0]) + states[0] * coefs[2]) * coefs[1]
@@ -309,15 +311,13 @@
     by_tiles(finish)
     await_all(4, s_recv.at[1], p_recv.at[1])
     carried_ref[...] = (unpack(p_recv.at[1]) + states[1] * coefs[2]) * coefs[1]
-    await_all(5, o_send, o_recv.at[0])
-    final_ref[...] = o_recv[0]
+    over_parts(lambda part, there: gradient_copy(part, there, part, there).wait_recv())
+    final_ref[...] = o_recv[...]
 
     for sent in ((0, e_send, e_recv.at[0]), (1, s_send, s_recv.at[0]), (2, g_send, g_recv),
-                 (3, e_recv.at[1], p_recv.at[0]), (4, s_recv.at[1], p_recv.at[1]), (5, o_send, o_recv.at[0])):
+                 (3, e_recv.at[1], p_recv.at[0]), (4, s_recv.at[1], p_recv.at[1])):
         await_sent(*sent)
-    if COMM:
-        for step in range(1, ndp):
-            dp_copy(step, True).wait_send()
+    over_parts(lambda part, there: gradient_copy(part, there, part, there).wait_send())
 
 
 def last_kernel(y_in, zlocal, wb_ref, carried_ref, final_ref, rate_ref, y_hbm, z_hbm, gres_hbm, gskip_hbm,
@@ -331,15 +331,11 @@
         copies[-1].start()
 
     send(y_in, y_hbm.at[0])
-    for q in range(channels // 256):
-        piece = slice(256 * q, 256 * q + 256)
-        product = times((wb_ref[0, :, piece], wb_ref[1, :, piece]), split(on_blocks(carried_ref[:, piece])))
-        z_ref[:, piece] = (zlocal[:, piece] + product).astype(bf16)
-        send(z_ref.at[:, piece], z_hbm.at[0, :, piece])
     lower_row = lax.broadcasted_iota(jnp.int32, (1, 128), 1) < 64
+    totals = jnp.sum(final_ref[...], axis=0)
     final = []
     for pair in range(channels // 128):
-        first, second = final_ref[2 * pair], final_ref[2 * pair + 1]
+        first, second = totals[2 * pair], totals[2 * pair + 1]
         gskip_ref[:, 128 * pair : 128 * pair + 128] = jnp.where(lower_row, pltpu.roll(first, 64, 1), second)
         final.append(jnp.where(lower_row, first, pltpu.roll(second, 64, 1)))
     send(gskip_ref, gskip_hbm)
@@ -355,6 +351,11 @@
     by_group += lax.dot_general(low, own_group, over_lanes, preferred_element_type=f32)
     gres_ref[...] = by_group * jnp.sqrt(1.0 - jnp.exp(-2.0 * rate_ref[...]))
     send(gres_ref, gres_hbm)
+    for q in range(channels // 256):
+        piece = slice(256 * q, 256 * q + 256)
+        product = times((wb_ref[0, :, piece], wb_ref[1, :, piece]), split(on_blocks(carried_ref[:, piece])))
+        z_ref[:, piece] = (zlocal[:, piece] + product).astype(bf16)
+        send(z_ref.at[:, piece], z_hbm.at[0, :, piece])
     for copy in copies:
         copy.wait()
 
@@ -388,7 +389,7 @@
             jax.ShapeDtypeStruct((rows, channels), f32),
             jax.ShapeDtypeStruct((2, rows, channels), bf16),
             jax.ShapeDtypeStruct((modes, channels), f32),
-            jax.ShapeDtypeStruct((nctx, 1, 128), f32),
+            jax.ShapeDtypeStruct((ndp, nctx, 1, 128), f32),
         ),
         in_specs=[hbm] * 8,
         out_specs=(vmem,) * 5,
@@ -416,15 +417,15 @@
             pltpu.VMEM((2, nctx, 8, 128), f32),
             pltpu.VMEM((nctx, 1, 128), f32),
             pltpu.VMEM((nctx, 1, 128), f32),
-            pltpu.VMEM((1, 128), f32),
             pltpu.VMEM((2, nctx, 8, 128), f32),
             pltpu.VMEM((1, 128), f32),
-            pltpu.VMEM((2, nctx, 1, 128), f32),
+            pltpu.VMEM((ndp, nctx, 1, 128), f32),
             pltpu.SemaphoreType.DMA((8,)),
-            pltpu.SemaphoreType.DMA((6, nctx)),
-            pltpu.SemaphoreType.DMA((6, nctx)),
-            pltpu.SemaphoreType.DMA((ndp,)),
-            pltpu.SemaphoreType.DMA((ndp,)),
+            pltpu.SemaphoreType.DMA((5, nctx)),
+            pltpu.SemaphoreType.DMA((5, nctx)),
+            pltpu.SemaphoreType.DMA((ndp, nctx)),
+            pltpu.SemaphoreType.DMA((ndp, nctx)),
+            pltpu.SemaphoreType.REGULAR,
         ],
         compiler_params=pltpu.CompilerParams(collective_id=0, has_side_effects=True, vmem_limit_bytes=32 * 1024 * 1024),
         name="hyena",

time: 42.6 us -> 45.3 us (1.063)
  Pallas kernels: 41.1 us -> 43.8 us
    pallas_call x1, Pallas kernels: 39.6 us -> 42.3 us  [shards(): pl.pallas_call(functools.partial(kernel, sizes), out_shape=(jax.ShapeDtyp...]
where the time goes in v4:
time: 45.3 us; the launch traced here: 45.1 us
  Pallas kernels  43.8 us (97%)
  local copies, waits for them, and re-layouts  0.69 us (2%)
  between operations  0.65 us (1%)
    pallas_call x1, Pallas kernels, shards(): pl.pallas_call(functools.partial(kernel, sizes), out_shape=(jax.ShapeDtyp...  42.3 us
    pallas_call x1, Pallas kernels, shards(): pl.pallas_call(last_kernel, out_shape=(jax.ShapeDtypeStruct(wide, bf16),...  1.45 us

profile of v4, /device:TPU:24, one launch (start us, length us, event | category | flops | bytes accessed | tf_op | source)
XLA Modules:
  0.0 45.1 jit_solution(2744311687840346953)
XLA Ops:
  0.6 42.3 %hyena.1 = (bf16[256,1024]{1,0:T(8,128)(2,1)S(1)}, f32[256,1024]{1,0:T(8,128)S(1)}, bf16[2,256,1024]{2,1,0:T(8,128)(2,1)S(1)}, f32[16,1024]{1,0:T(8,128)S(1)}, f32[4,16,1,128]{3,2,1,0:T(1,128)S(1)}) custom-call(bf16[1,256,1024]{2,1,0:T(8,128)(2,1)} %x_hbm.1, bf16[1,256,1024]{2,1,0:T(8,128)(2,1)} %d_hbm.1, f32[16,64]{1,0:T(8,128)} %bitcast.7, ...), custom_call_target="tpu_custom_call" | custom-call | tf_op jit(solution)/shard_map/hyena/pallas_call | solution.py:385
  43.0 0.0 copy-start
  43.0 0.7 %copy-done = f32[64,16]{0,1:T(8,128)S(1)} copy-done((f32[64,16]{0,1:T(8,128)S(1)}, f32[64,16]{0,1:T(8,128)}, u32[]{:S(2)}) %copy-start) | copy-done | bytes 4120
  43.7 1.4 %last.1 = (bf16[1,256,1024]{2,1,0:T(8,128)(2,1)}, bf16[1,256,1024]{2,1,0:T(8,128)(2,1)}, f32[16,64]{1,0:T(8,128)}, f32[1,1024]{1,0:T(1,128)}) custom-call(bf16[256,1024]{1,0:T(8,128)(2,1)S(1)} %get-tuple-element.13.y_in, f32[256,1024]{1,0:T(8,128)S(1)} %get-tuple-element.14.zlocal, bf16[2,256,1024]{2,1,0:T(8,128)(2,1)S(1)} %get-tuple-element.15.wb_ref, ...), custom_call_target="tpu_custom_call" | custom-call | tf_op jit(solution)/shard_map/last/pallas_call | solution.py:433
Async XLA Ops:
  43.0 0.7 %copy-start = (f32[64,16]{0,1:T(8,128)S(1)}, f32[64,16]{0,1:T(8,128)}, u32[]{:S(2)}) copy-start(f32[64,16]{0,1:T(8,128)} %param.11) | copy-start | bytes 12292

commit v5 on v3

--- a/solution.py
+++ b/solution.py
@@ -51,10 +51,11 @@
 
 
 def kernel(sizes, x_hbm, d_hbm, res_hbm, rate_hbm, skip_hbm, fwd_hbm, inv_hbm, trig_hbm,
-           y_ref, zlocal, wb_ref, carried_ref, final_ref,
+           y_ref, z_ref, final_ref, weight_ref, chosen_ref,
            x_ref, d_ref, res_ref, rate_ref, skip_ref, fwd_ref, inv_ref, trig_ref,
-           wf_ref, h_ref, x_hat, d_hat, ylocal, rate_row, states, coefs, packs, e_send, e_recv, s_send, s_recv,
-           g_send, g_recv, p_send, p_recv, o_send, o_recv, load_sem, send_sem, recv_sem, psend_sem, precv_sem):
+           wf_ref, wb_ref, h_ref, x_hat, d_hat, ylocal, zlocal, rate_row, states, coefs, carried_ref, packs,
+           out_send, out_recv, back_send, back_recv, p_send, from_dp, o_send, o_recv,
+           load_sem, send_sem, recv_sem, psend_sem, precv_sem):
     nctx, ndp, rows, channels, groups, modes, scale = sizes
     half = rows // 2
     tiles = channels // 256
@@ -63,12 +64,16 @@
 
     barrier = pltpu.get_barrier_semaphore()
 
-    def greet(step, carried):
+    def far_first(count):
+        return nctx // 2 + jnp.where(count % 2 == 1, -((count + 1) // 2), count // 2)
+
+    def greet(count, carried):
+        step = far_first(count)
         pl.semaphore_signal(barrier, inc=1, device_id={"ctx": lax.rem(me + step, nctx)}, device_id_type=MESH)
         return carried
 
     if COMM:
-        lax.fori_loop(1, nctx, greet, 0)
+        lax.fori_loop(0, nctx - 1, greet, 0)
         for step in range(1, ndp):
             pl.semaphore_signal(barrier, inc=1, device_id={"dp": lax.rem(mine + step, ndp)}, device_id_type=MESH)
 
@@ -104,17 +109,17 @@
 
             lax.fori_loop(0, tiles, turn, 0)
 
-    def pack(array, target):
+    def pack(array, target, top):
         for pair in range(nctx // 2):
             low = array[0:8, 128 * pair : 128 * pair + 128]
             high = array[8:16, 128 * pair : 128 * pair + 128]
-            target[2 * pair] = jnp.where(lower, low, pltpu.roll(high, 64, 1))
-            target[2 * pair + 1] = jnp.where(lower, pltpu.roll(low, 64, 1), high)
-
-    def unpack(source):
+            target[2 * pair, top : top + 8] = jnp.where(lower, low, pltpu.roll(high, 64, 1))
+            target[2 * pair + 1, top : top + 8] = jnp.where(lower, pltpu.roll(low, 64, 1), high)
+
+    def unpack(source, top):
         lows, highs = [], []
         for pair in range(nctx // 2):
-            first, second = source[2 * pair], source[2 * pair + 1]
+            first, second = source[2 * pair, top : top + 8], source[2 * pair + 1, top : top + 8]
             lows.append(jnp.where(lower, first, pltpu.roll(second, 64, 1)))
             highs.append(jnp.where(lower, pltpu.roll(first, 64, 1), second))
         return jnp.concatenate([jnp.concatenate(lows, axis=1), jnp.concatenate(highs, axis=1)], axis=0)
@@ -138,14 +143,14 @@
 
     loads[2].wait()
     by_tiles(end_states)
-    pack(states[0], e_send)
+    pack(states[0], out_send, 0)
     loads[3].wait()
     by_tiles(start_states)
-    pack(states[1], s_send)
+    pack(states[1], out_send, 8)
 
     def state_copy(there, kind, send, recv, slot_there):
         return pltpu.make_async_remote_copy(
-            src_ref=send.at[there] if kind < 5 else send,
+            src_ref=send.at[there] if kind < 2 else send,
             dst_ref=recv.at[slot_there],
             send_sem=send_sem.at[kind, there],
             recv_sem=recv_sem.at[kind, slot_there],
@@ -163,8 +168,7 @@
 
     def send_all(kind, send, recv):
         def turn(count, carried):
-            step = nctx // 2 + jnp.where(count % 2 == 1, -((count + 1) // 2), count // 2)
-            state_copy(lax.rem(me + step, nctx), kind, send, recv, me).start()
+            state_copy(lax.rem(me + far_first(count), nctx), kind, send, recv, me).start()
             return carried
 
         if COMM:
@@ -202,19 +206,15 @@
         for part in range(2):
             pair = 2 * q + part
             grad_row, skip_row = grad_piece[:, 128 * part : 128 * part + 128], skip_piece[:, 128 * part : 128 * part + 128]
-            g_send[2 * pair] = jnp.where(lower_row, grad_row, pltpu.roll(skip_row, 64, 1))
-            g_send[2 * pair + 1] = jnp.where(lower_row, pltpu.roll(grad_row, 64, 1), skip_row)
+            out_send[2 * pair, 16:17] = jnp.where(lower_row, grad_row, pltpu.roll(skip_row, 64, 1))
+            out_send[2 * pair + 1, 16:17] = jnp.where(lower_row, pltpu.roll(grad_row, 64, 1), skip_row)
 
     by_tiles(spectra)
 
     if COMM:
         pl.semaphore_wait(barrier, nctx - 1 + ndp - 1)
-    send_all(0, e_send, e_recv.at[0])
-    send_all(2, g_send, g_recv)
-    send_all(1, s_send, s_recv.at[0])
-    e_recv[0, me] = e_send[me]
-    s_recv[0, me] = s_send[me]
-    g_recv[me] = g_send[me]
+    send_all(0, out_send, out_recv)
+    out_recv[me] = out_send[me]
 
     loads[1].wait()
     coefs[0] = times_row(res_ref[...], own_group) * jnp.sqrt(1.0 - jnp.exp(-2.0 * rate_wide))
@@ -223,9 +223,14 @@
     inverse_wide = 1.0 / (1.0 + block_wide)
     coefs[1] = coefs[0] * step_wide
     coefs[2] = inverse_wide
-    pack(block_wide, packs.at[0])
-    pack(inverse_wide, packs.at[1])
-    pack(step_wide, packs.at[2])
+    pack(block_wide, packs.at[0], 0)
+    pack(inverse_wide, packs.at[1], 0)
+    pack(step_wide, packs.at[2], 0)
+
+    weight_ref[...] = jnp.sqrt(1.0 - jnp.exp(-2.0 * rate_ref[...]))
+    chosen_ref[...] = (
+        lax.broadcasted_iota(jnp.int32, (channels, groups), 0) // modes == lax.broadcasted_iota(jnp.int32, (channels, groups), 1)
+    ).astype(bf16)
 
     def own_part(q, piece):
         response = times(split(h_ref[:, piece]), split(on_blocks(coefs[0, :, piece])))
@@ -240,36 +245,33 @@
     by_tiles(own_part)
 
     block_own, inverse_own, step_own = packs[0, me], packs[1, me], packs[2, me]
-    await_all(0, e_send, e_recv.at[0])
-    running = jnp.zeros((8, 128), f32)
-    for block in range(nctx):
-        e_recv[1, block] = running
-        running = running * block_own + e_recv[0, block]
-    send_all(3, e_recv.at[1], p_recv.at[0])
-    p_recv[0, me] = e_recv[1, me]
-    await_all(2, g_send, g_recv)
-    gradient = g_recv[0]
-    for block in range(1, nctx):
-        gradient += g_recv[block]
-    await_all(1, s_send, s_recv.at[0])
-    running = jnp.zeros((8, 128), f32)
-    owned = jnp.zeros((8, 128), f32)
-    for block in range(nctx - 1, -1, -1):
-        s_recv[1, block] = running
-        start = s_recv[0, block]
-        running = running * block_own + start
-        owned += start * (e_recv[1, block] + e_recv[0, block] * inverse_own)
-    high, low = split(owned * step_own)
     lane_row = lax.broadcasted_iota(jnp.int32, (128, 128), 0)
     lane_column = lax.broadcasted_iota(jnp.int32, (128, 128), 1)
     chosen = (
         (lane_row // 64 == (lane_column % 16) // 8) & ((lane_row % 64) // 16 == lane_column // 16)
     ).astype(bf16)
+    right_row = lax.broadcasted_iota(jnp.int32, (8, 128), 0) == lanes % 8
+    await_all(0, out_send, out_recv)
+    running = jnp.zeros((8, 128), f32)
+    inner = []
+    for block in range(nctx):
+        end = out_recv[block, 0:8]
+        back_send[block, 0:8] = running
+        inner.append(running + end * inverse_own)
+        running = running * block_own + end
+    running = jnp.zeros((8, 128), f32)
+    owned = jnp.zeros((8, 128), f32)
+    gradient = jnp.zeros((1, 128), f32)
+    for block in range(nctx - 1, -1, -1):
+        start = out_recv[block, 8:16]
+        back_send[block, 8:16] = running
+        running = running * block_own + start
+        owned += start * inner[block]
+        gradient += out_recv[block, 16:17]
+    high, low = split(owned * step_own)
     summed = jnp.dot(high, chosen, preferred_element_type=f32) + jnp.dot(low, chosen, preferred_element_type=f32)
-    right_row = lax.broadcasted_iota(jnp.int32, (8, 128), 0) == lanes % 8
     gradient += jnp.sum(jnp.where(right_row & lower, summed, 0.0), axis=0, keepdims=True)
     p_send[...] = gradient
-    from_dp = o_recv.at[1]
 
     def dp_copy(step, here):
         there = lax.rem(mine + step, ndp)
@@ -286,8 +288,8 @@
     if COMM:
         for step in range(1, ndp):
             dp_copy(step, False).start()
-    send_all(4, s_recv.at[1], p_recv.at[1])
-    p_recv[1, me] = s_recv[1, me]
+    send_all(1, back_send, back_recv)
+    back_recv[me] = back_send[me]
     from_dp[mine] = gradient
     if COMM:
         for step in range(1, ndp):
@@ -296,34 +298,32 @@
     for other in range(1, ndp):
         gradient += from_dp[other]
     o_send[...] = gradient * scale
-    send_all(5, o_send, o_recv.at[0])
-    o_recv[0, me] = gradient * scale
-
-    await_all(3, e_recv.at[1], p_recv.at[0])
-    carried_ref[...] = (unpack(p_recv.at[0]) + states[0] * coefs[2]) * coefs[1]
+    send_all(2, o_send, o_recv)
+    o_recv[me] = gradient * scale
+
+    await_all(1, back_send, back_recv)
+    carried_ref[0] = (unpack(back_recv, 0) + states[0] * coefs[2]) * coefs[1]
+    carried_ref[1] = (unpack(back_recv, 8) + states[1] * coefs[2]) * coefs[1]
 
     def finish(q, piece):
-        product = times((wf_ref[0, :, piece], wf_ref[1, :, piece]), split(on_blocks(carried_ref[:, piece])))
+        product = times((wf_ref[0, :, piece], wf_ref[1, :, piece]), split(on_blocks(carried_ref[0, :, piece])))
         y_ref[:, piece] = (ylocal[:, piece] + product).astype(bf16)
+        product = times((wb_ref[0, :, piece], wb_ref[1, :, piece]), split(on_blocks(carried_ref[1, :, piece])))
+        z_ref[:, piece] = (zlocal[:, piece] + product).astype(bf16)
 
     by_tiles(finish)
-    await_all(4, s_recv.at[1], p_recv.at[1])
-    carried_ref[...] = (unpack(p_recv.at[1]) + states[1] * coefs[2]) * coefs[1]
-    await_all(5, o_send, o_recv.at[0])
-    final_ref[...] = o_recv[0]
-
-    for sent in ((0, e_send, e_recv.at[0]), (1, s_send, s_recv.at[0]), (2, g_send, g_recv),
-                 (3, e_recv.at[1], p_recv.at[0]), (4, s_recv.at[1], p_recv.at[1]), (5, o_send, o_recv.at[0])):
+    for sent in ((0, out_send, out_recv), (1, back_send, back_recv), (2, o_send, o_recv)):
         await_sent(*sent)
     if COMM:
         for step in range(1, ndp):
             dp_copy(step, True).wait_send()
-
-
-def last_kernel(y_in, zlocal, wb_ref, carried_ref, final_ref, rate_ref, y_hbm, z_hbm, gres_hbm, gskip_hbm,
-                z_ref, gres_ref, gskip_ref, sem):
-    channels = zlocal.shape[1]
-    modes, groups = rate_ref.shape
+    await_all(2, o_send, o_recv)
+    final_ref[...] = o_recv[...]
+
+
+def last_kernel(y_in, z_in, final_ref, weight_ref, chosen_ref, y_hbm, z_hbm, gres_hbm, gskip_hbm, gres_ref, gskip_ref, sem):
+    channels = y_in.shape[1]
+    modes = weight_ref.shape[0]
     copies = []
 
     def send(source, target):
@@ -331,11 +331,7 @@
         copies[-1].start()
 
     send(y_in, y_hbm.at[0])
-    for q in range(channels // 256):
-        piece = slice(256 * q, 256 * q + 256)
-        product = times((wb_ref[0, :, piece], wb_ref[1, :, piece]), split(on_blocks(carried_ref[:, piece])))
-        z_ref[:, piece] = (zlocal[:, piece] + product).astype(bf16)
-        send(z_ref.at[:, piece], z_hbm.at[0, :, piece])
+    send(z_in, z_hbm.at[0])
     lower_row = lax.broadcasted_iota(jnp.int32, (1, 128), 1) < 64
     final = []
     for pair in range(channels // 128):
@@ -343,17 +339,13 @@
         gskip_ref[:, 128 * pair : 128 * pair + 128] = jnp.where(lower_row, pltpu.roll(first, 64, 1), second)
         final.append(jnp.where(lower_row, first, pltpu.roll(second, 64, 1)))
     send(gskip_ref, gskip_hbm)
-    own_group = (
-        lax.broadcasted_iota(jnp.int32, (groups, channels), 1) // modes == lax.broadcasted_iota(jnp.int32, (groups, channels), 0)
-    ).astype(bf16)
     own_mode = (
         lax.broadcasted_iota(jnp.int32, (modes, channels), 1) % modes == lax.broadcasted_iota(jnp.int32, (modes, channels), 0)
     )
     high, low = split(jnp.where(own_mode, jnp.concatenate(final, axis=1), 0.0))
-    over_lanes = (((1,), (1,)), ((), ()))
-    by_group = lax.dot_general(high, own_group, over_lanes, preferred_element_type=f32)
-    by_group += lax.dot_general(low, own_group, over_lanes, preferred_element_type=f32)
-    gres_ref[...] = by_group * jnp.sqrt(1.0 - jnp.exp(-2.0 * rate_ref[...]))
+    chosen = chosen_ref[...]
+    by_group = jnp.dot(high, chosen, preferred_element_type=f32) + jnp.dot(low, chosen, preferred_element_type=f32)
+    gres_ref[...] = by_group * weight_ref[...]
     send(gres_ref, gres_hbm)
     for copy in copies:
         copy.wait()
@@ -385,10 +377,10 @@
         functools.partial(kernel, sizes),
         out_shape=(
             jax.ShapeDtypeStruct((rows, channels), bf16),
-            jax.ShapeDtypeStruct((rows, channels), f32),
-            jax.ShapeDtypeStruct((2, rows, channels), bf16),
-            jax.ShapeDtypeStruct((modes, channels), f32),
+            jax.ShapeDtypeStruct((rows, channels), bf16),
             jax.ShapeDtypeStruct((nctx, 1, 128), f32),
+            jax.ShapeDtypeStruct((modes, groups), f32),
+            jax.ShapeDtypeStruct((channels, groups), bf16),
         ),
         in_specs=[hbm] * 8,
         out_specs=(vmem,) * 5,
@@ -402,6 +394,8 @@
             pltpu.VMEM((2, rows, rows), bf16),
             pltpu.VMEM((rows // 2, 128), f32),
             pltpu.VMEM((2, rows, channels), bf16),
+            pltpu.VMEM((2, rows, channels), bf16),
+            pltpu.VMEM((rows, channels), f32),
             pltpu.VMEM((rows, channels), f32),
             pltpu.VMEM((rows, channels), f32),
             pltpu.VMEM((rows, channels), f32),
@@ -409,20 +403,19 @@
             pltpu.VMEM((1, channels), f32),
             pltpu.VMEM((2, modes, channels), f32),
             pltpu.VMEM((3, modes, channels), f32),
+            pltpu.VMEM((2, modes, channels), f32),
             pltpu.VMEM((3, nctx, 8, 128), f32),
-            pltpu.VMEM((nctx, 8, 128), f32),
-            pltpu.VMEM((2, nctx, 8, 128), f32),
-            pltpu.VMEM((nctx, 8, 128), f32),
-            pltpu.VMEM((2, nctx, 8, 128), f32),
+            pltpu.VMEM((nctx, 17, 128), f32),
+            pltpu.VMEM((nctx, 17, 128), f32),
+            pltpu.VMEM((nctx, 16, 128), f32),
+            pltpu.VMEM((nctx, 16, 128), f32),
+            pltpu.VMEM((1, 128), f32),
+            pltpu.VMEM((ndp, 1, 128), f32),
+            pltpu.VMEM((1, 128), f32),
             pltpu.VMEM((nctx, 1, 128), f32),
-            pltpu.VMEM((nctx, 1, 128), f32),
-            pltpu.VMEM((1, 128), f32),
-            pltpu.VMEM((2, nctx, 8, 128), f32),
-            pltpu.VMEM((1, 128), f32),
-            pltpu.VMEM((2, nctx, 1, 128), f32),
             pltpu.SemaphoreType.DMA((8,)),
-            pltpu.SemaphoreType.DMA((6, nctx)),
-            pltpu.SemaphoreType.DMA((6, nctx)),
+            pltpu.SemaphoreType.DMA((3, nctx)),
+            pltpu.SemaphoreType.DMA((3, nctx)),
             pltpu.SemaphoreType.DMA((ndp,)),
             pltpu.SemaphoreType.DMA((ndp,)),
         ],
@@ -437,17 +430,16 @@
             jax.ShapeDtypeStruct((modes, groups), f32),
             jax.ShapeDtypeStruct((1, channels), f32),
         ),
-        in_specs=[vmem] * 6,
+        in_specs=[vmem] * 5,
         out_specs=(hbm,) * 4,
         scratch_shapes=[
-            pltpu.VMEM((rows, channels), bf16),
             pltpu.VMEM((modes, groups), f32),
             pltpu.VMEM((1, channels), f32),
-            pltpu.SemaphoreType.DMA((3 + channels // 256,)),
+            pltpu.SemaphoreType.DMA((4,)),
         ],
         compiler_params=pltpu.CompilerParams(vmem_limit_bytes=32 * 1024 * 1024),
         name="last",
-    )(*parts, decay_rates.T)
+    )(*parts)
     return outputs, grad_inputs, grad_residues.T, grad_skip.reshape(channels)
 
 

time: 42.6 us -> 37.9 us (0.89)
  Pallas kernels: 41.1 us -> 37.2 us
  local copies, waits for them, and re-layouts: 0.69 us -> 0 us
    pallas_call x1, Pallas kernels: 39.6 us -> 36.2 us  [shards(): pl.pallas_call(functools.partial(kernel, sizes), out_shape=(jax.ShapeDtyp...]
    unnamed x2 -> x0, local copies, waits for them, and re-layouts: 0.69 us -> none
    pallas_call x1, Pallas kernels: 1.44 us -> 1.01 us  [shards(): pl.pallas_call(last_kernel, out_shape=(jax.ShapeDtypeStruct(wide, bf16),...]
where the time goes in v5:
time: 37.9 us; the launch traced here: 37.8 us
  Pallas kernels  37.2 us (98%)
  between operations  0.64 us (2%)
    pallas_call x1, Pallas kernels, shards(): pl.pallas_call(functools.partial(kernel, sizes), out_shape=(jax.ShapeDtyp...  36.2 us
    pallas_call x1, Pallas kernels, shards(): pl.pallas_call(last_kernel, out_shape=(jax.ShapeDtypeStruct(wide, bf16),...  1.01 us

profile of v5, /device:TPU:24, one launch (start us, length us, event | category | flops | bytes accessed | tf_op | source)
XLA Modules:
  0.0 37.8 jit_solution(16215957018524101523)
XLA Ops:
  0.6 36.2 %hyena.1 = (bf16[256,1024]{1,0:T(8,128)(2,1)S(1)}, bf16[256,1024]{1,0:T(8,128)(2,1)S(1)}, f32[16,1,128]{2,1,0:T(1,128)S(1)}, f32[16,64]{1,0:T(8,128)S(1)}, bf16[1024,64]{1,0:T(8,128)(2,1)S(1)}) custom-call(bf16[1,256,1024]{2,1,0:T(8,128)(2,1)} %x_hbm.1, bf16[1,256,1024]{2,1,0:T(8,128)(2,1)} %d_hbm.1, f32[16,64]{1,0:T(8,128)} %bitcast.5, f32[16,64]{1,0:T(8,128)} %bitcast.6, ...), custom_call_target="tpu_custom_call" | custom-call | tf_op jit(solution)/shard_map/hyena/pallas_call | solution.py:376
  36.8 1.0 %last.1 = (bf16[1,256,1024]{2,1,0:T(8,128)(2,1)}, bf16[1,256,1024]{2,1,0:T(8,128)(2,1)}, f32[16,64]{1,0:T(8,128)}, f32[1,1024]{1,0:T(1,128)}) custom-call(bf16[256,1024]{1,0:T(8,128)(2,1)S(1)} %get-tuple-element.13.y_in, bf16[256,1024]{1,0:T(8,128)(2,1)S(1)} %get-tuple-element.14.z_in, f32[16,1,128]{2,1,0:T(1,128)S(1)} %get-tuple-element.15.final_ref, ...), custom_call_target="tpu_custom_call" | custom-call | tf_op jit(solution)/shard_map/last/pallas_call | solution.py:425

commit v6 on v5

--- a/solution.py
+++ b/solution.py
@@ -213,7 +213,12 @@
 
     if COMM:
         pl.semaphore_wait(barrier, nctx - 1 + ndp - 1)
-    send_all(0, out_send, out_recv)
+    second = lax.rem(lax.axis_index("tp"), 2) == 1
+
+    @pl.when(jnp.logical_not(second))
+    def _():
+        send_all(0, out_send, out_recv)
+
     out_recv[me] = out_send[me]
 
     loads[1].wait()
@@ -243,6 +248,11 @@
         zlocal[:, piece] = times((inv_ref[0], inv_ref[1]), split(z_hat)) + skip * d_ref[:, piece].astype(f32)
 
     by_tiles(own_part)
+
+    @pl.when(second)
+    def _():
+        send_all(0, out_send, out_recv)
+
 
     block_own, inverse_own, step_own = packs[0, me], packs[1, me], packs[2, me]
     lane_row = lax.broadcasted_iota(jnp.int32, (128, 128), 0)

time: 37.9 us -> 38.4 us (1.013)
  the two profiles are of different devices: /device:TPU:24 before, /device:TPU:1 now
where the time goes in v6:
time: 38.4 us; the launch traced here: 38.3 us
  Pallas kernels  37.6 us (98%)
  between operations  0.64 us (2%)
    pallas_call x1, Pallas kernels, shards(): pl.pallas_call(functools.partial(kernel, sizes), out_shape=(jax.ShapeDtyp...  36.6 us
    pallas_call x1, Pallas kernels, shards(): pl.pallas_call(last_kernel, out_shape=(jax.ShapeDtypeStruct(wide, bf16),...  1.01 us

profile of v6, /device:TPU:1, one launch (start us, length us, event | category | flops | bytes accessed | tf_op | source)
XLA Modules:
  0.0 38.3 jit_solution(16359564898602127680)
XLA Ops:
  0.6 36.6 %hyena.1 = (bf16[256,1024]{1,0:T(8,128)(2,1)S(1)}, bf16[256,1024]{1,0:T(8,128)(2,1)S(1)}, f32[16,1,128]{2,1,0:T(1,128)S(1)}, f32[16,64]{1,0:T(8,128)S(1)}, bf16[1024,64]{1,0:T(8,128)(2,1)S(1)}) custom-call(bf16[1,256,1024]{2,1,0:T(8,128)(2,1)} %x_hbm.1, bf16[1,256,1024]{2,1,0:T(8,128)(2,1)} %d_hbm.1, f32[16,64]{1,0:T(8,128)} %bitcast.5, f32[16,64]{1,0:T(8,128)} %bitcast.6, ...), custom_call_target="tpu_custom_call" | custom-call | tf_op jit(solution)/shard_map/hyena/pallas_call | solution.py:386
  37.3 1.0 %last.1 = (bf16[1,256,1024]{2,1,0:T(8,128)(2,1)}, bf16[1,256,1024]{2,1,0:T(8,128)(2,1)}, f32[16,64]{1,0:T(8,128)}, f32[1,1024]{1,0:T(1,128)}) custom-call(bf16[256,1024]{1,0:T(8,128)(2,1)S(1)} %get-tuple-element.13.y_in, bf16[256,1024]{1,0:T(8,128)(2,1)S(1)} %get-tuple-element.14.z_in, f32[16,1,128]{2,1,0:T(1,128)S(1)} %get-tuple-element.15.final_ref, ...), custom_call_target="tpu_custom_call" | custom-call | tf_op jit(solution)/shard_map/last/pallas_call | solution.py:435

commit v7 on v5

--- a/solution.py
+++ b/solution.py
@@ -54,8 +54,8 @@
            y_ref, z_ref, final_ref, weight_ref, chosen_ref,
            x_ref, d_ref, res_ref, rate_ref, skip_ref, fwd_ref, inv_ref, trig_ref,
            wf_ref, wb_ref, h_ref, x_hat, d_hat, ylocal, zlocal, rate_row, states, coefs, carried_ref, packs,
-           out_send, out_recv, back_send, back_recv, p_send, from_dp, o_send, o_recv,
-           load_sem, send_sem, recv_sem, psend_sem, precv_sem):
+           out_send, out_recv, back_send, back_recv, o_send, o_recv,
+           load_sem, send_sem, recv_sem, osend_sem, orecv_sem, ring_sem):
     nctx, ndp, rows, channels, groups, modes, scale = sizes
     half = rows // 2
     tiles = channels // 256
@@ -150,7 +150,7 @@
 
     def state_copy(there, kind, send, recv, slot_there):
         return pltpu.make_async_remote_copy(
-            src_ref=send.at[there] if kind < 2 else send,
+            src_ref=send.at[there],
             dst_ref=recv.at[slot_there],
             send_sem=send_sem.at[kind, there],
             recv_sem=recv_sem.at[kind, slot_there],
@@ -159,12 +159,12 @@
         )
 
     def over_peers(body):
-        def turn(step, carried):
-            body(lax.rem(me + step, nctx))
+        def turn(count, carried):
+            body(lax.rem(me + far_first(nctx - 2 - count), nctx))
             return carried
 
         if COMM:
-            lax.fori_loop(1, nctx, turn, 0)
+            lax.fori_loop(0, nctx - 1, turn, 0)
 
     def send_all(kind, send, recv):
         def turn(count, carried):
@@ -213,6 +213,8 @@
 
     if COMM:
         pl.semaphore_wait(barrier, nctx - 1 + ndp - 1)
+        for step in range(1, ndp):
+            pl.semaphore_signal(ring_sem, inc=1, device_id={"dp": lax.rem(mine + step, ndp)}, device_id_type=MESH)
     send_all(0, out_send, out_recv)
     out_recv[me] = out_send[me]
 
@@ -268,38 +270,36 @@
         running = running * block_own + start
         owned += start * inner[block]
         gradient += out_recv[block, 16:17]
+    send_all(1, back_send, back_recv)
+    back_recv[me] = back_send[me]
     high, low = split(owned * step_own)
     summed = jnp.dot(high, chosen, preferred_element_type=f32) + jnp.dot(low, chosen, preferred_element_type=f32)
     gradient += jnp.sum(jnp.where(right_row & lower, summed, 0.0), axis=0, keepdims=True)
-    p_send[...] = gradient
-
-    def dp_copy(step, here):
-        there = lax.rem(mine + step, ndp)
-        slot = there if here else mine
+    gradient = gradient * scale
+    o_send[...] = gradient
+    o_recv[mine * nctx + me] = gradient
+
+    def gradient_copy(offset, step):
+        part, there = lax.rem(mine + offset, ndp), lax.rem(me + step, nctx)
         return pltpu.make_async_remote_copy(
-            src_ref=p_send,
-            dst_ref=from_dp.at[slot],
-            send_sem=psend_sem.at[there],
-            recv_sem=precv_sem.at[slot],
-            device_id={"dp": there},
+            src_ref=o_send,
+            dst_ref=o_recv.at[mine * nctx + me],
+            send_sem=osend_sem,
+            recv_sem=orecv_sem,
+            device_id={"dp": part, "ctx": there},
             device_id_type=MESH,
         )
 
+    def send_gradients(count, carried):
+        for offset in range(ndp):
+            gradient_copy(offset, far_first(count)).start()
+        return carried
+
     if COMM:
-        for step in range(1, ndp):
-            dp_copy(step, False).start()
-    send_all(1, back_send, back_recv)
-    back_recv[me] = back_send[me]
-    from_dp[mine] = gradient
-    if COMM:
-        for step in range(1, ndp):
-            dp_copy(step, True).wait_recv()
-    gradient = from_dp[0]
-    for other in range(1, ndp):
-        gradient += from_dp[other]
-    o_send[...] = gradient * scale
-    send_all(2, o_send, o_recv)
-    o_recv[me] = gradient * scale
+        pl.semaphore_wait(ring_sem, ndp - 1)
+        lax.fori_loop(0, nctx - 1, send_gradients, 0)
+        for offset in range(1, ndp):
+            gradient_copy(offset, 0).start()
 
     await_all(1, back_send, back_recv)
     carried_ref[0] = (unpack(back_recv, 0) + states[0] * coefs[2]) * coefs[1]
@@ -312,13 +312,25 @@
         z_ref[:, piece] = (zlocal[:, piece] + product).astype(bf16)
 
     by_tiles(finish)
-    for sent in ((0, out_send, out_recv), (1, back_send, back_recv), (2, o_send, o_recv)):
+    for sent in ((0, out_send, out_recv), (1, back_send, back_recv)):
         await_sent(*sent)
     if COMM:
-        for step in range(1, ndp):
-            dp_copy(step, True).wait_send()
-    await_all(2, o_send, o_recv)
-    final_ref[...] = o_recv[...]
+        others = o_recv.at[pl.ds(0, ndp * nctx - 1)]
+        everything = pltpu.make_async_remote_copy(
+            src_ref=others,
+            dst_ref=others,
+            send_sem=osend_sem,
+            recv_sem=orecv_sem,
+            device_id={"ctx": lax.rem(me + 1, nctx)},
+            device_id_type=MESH,
+        )
+        everything.wait_send()
+        everything.wait_recv()
+    for owner in range(nctx):
+        total = o_recv[owner]
+        for part in range(1, ndp):
+            total += o_recv[part * nctx + owner]
+        final_ref[owner] = total
 
 
 def last_kernel(y_in, z_in, final_ref, weight_ref, chosen_ref, y_hbm, z_hbm, gres_hbm, gskip_hbm, gres_ref, gskip_ref, sem):
@@ -410,14 +422,13 @@
             pltpu.VMEM((nctx, 16, 128), f32),
             pltpu.VMEM((nctx, 16, 128), f32),
             pltpu.VMEM((1, 128), f32),
-            pltpu.VMEM((ndp, 1, 128), f32),
-            pltpu.VMEM((1, 128), f32),
-            pltpu.VMEM((nctx, 1, 128), f32),
+            pltpu.VMEM((ndp * nctx, 1, 128), f32),
             pltpu.SemaphoreType.DMA((8,)),
-            pltpu.SemaphoreType.DMA((3, nctx)),
-            pltpu.SemaphoreType.DMA((3, nctx)),
-            pltpu.SemaphoreType.DMA((ndp,)),
-            pltpu.SemaphoreType.DMA((ndp,)),
+            pltpu.SemaphoreType.DMA((2, nctx)),
+            pltpu.SemaphoreType.DMA((2, nctx)),
+            pltpu.SemaphoreType.DMA,
+            pltpu.SemaphoreType.DMA,
+            pltpu.SemaphoreType.REGULAR,
         ],
         compiler_params=pltpu.CompilerParams(collective_id=0, has_side_effects=True, vmem_limit_bytes=32 * 1024 * 1024),
         name="hyena",

time: 37.9 us -> 38.4 us (1.013)
  Pallas kernels: 37.2 us -> 37.6 us
    pallas_call x1, Pallas kernels: 36.2 us -> 36.6 us  [shards(): pl.pallas_call(functools.partial(kernel, sizes), out_shape=(jax.ShapeDtyp...]
where the time goes in v7:
time: 38.4 us; the launch traced here: 38.3 us
  Pallas kernels  37.6 us (98%)
  between operations  0.64 us (2%)
    pallas_call x1, Pallas kernels, shards(): pl.pallas_call(functools.partial(kernel, sizes), out_shape=(jax.ShapeDtyp...  36.6 us
    pallas_call x1, Pallas kernels, shards(): pl.pallas_call(last_kernel, out_shape=(jax.ShapeDtypeStruct(wide, bf16),...  1.01 us

profile of v7, /device:TPU:24, one launch (start us, length us, event | category | flops | bytes accessed | tf_op | source)
XLA Modules:
  0.0 38.3 jit_solution(5906149608250485447)
XLA Ops:
  0.6 36.6 %hyena.1 = (bf16[256,1024]{1,0:T(8,128)(2,1)S(1)}, bf16[256,1024]{1,0:T(8,128)(2,1)S(1)}, f32[16,1,128]{2,1,0:T(1,128)S(1)}, f32[16,64]{1,0:T(8,128)S(1)}, bf16[1024,64]{1,0:T(8,128)(2,1)S(1)}) custom-call(bf16[1,256,1024]{2,1,0:T(8,128)(2,1)} %x_hbm.1, bf16[1,256,1024]{2,1,0:T(8,128)(2,1)} %d_hbm.1, f32[16,64]{1,0:T(8,128)} %bitcast.5, f32[16,64]{1,0:T(8,128)} %bitcast.6, ...), custom_call_target="tpu_custom_call" | custom-call | tf_op jit(solution)/shard_map/hyena/pallas_call | solution.py:388
  37.3 1.0 %last.1 = (bf16[1,256,1024]{2,1,0:T(8,128)(2,1)}, bf16[1,256,1024]{2,1,0:T(8,128)(2,1)}, f32[16,64]{1,0:T(8,128)}, f32[1,1024]{1,0:T(1,128)}) custom-call(bf16[256,1024]{1,0:T(8,128)(2,1)S(1)} %get-tuple-element.13.y_in, bf16[256,1024]{1,0:T(8,128)(2,1)S(1)} %get-tuple-element.14.z_in, f32[16,1,128]{2,1,0:T(1,128)S(1)} %get-tuple-element.15.final_ref, ...), custom_call_target="tpu_custom_call" | custom-call | tf_op jit(solution)/shard_map/last/pallas_call | solution.py:436

commit v8 on v7

--- a/solution.py
+++ b/solution.py
@@ -301,6 +301,8 @@
         for offset in range(1, ndp):
             gradient_copy(offset, 0).start()
 
+    for sent in ((0, out_send, out_recv), (1, back_send, back_recv)):
+        await_sent(*sent)
     await_all(1, back_send, back_recv)
     carried_ref[0] = (unpack(back_recv, 0) + states[0] * coefs[2]) * coefs[1]
     carried_ref[1] = (unpack(back_recv, 8) + states[1] * coefs[2]) * coefs[1]
@@ -312,8 +314,6 @@
         z_ref[:, piece] = (zlocal[:, piece] + product).astype(bf16)
 
     by_tiles(finish)
-    for sent in ((0, out_send, out_recv), (1, back_send, back_recv)):
-        await_sent(*sent)
     if COMM:
         others = o_recv.at[pl.ds(0, ndp * nctx - 1)]
         everything = pltpu.make_async_remote_copy(

time: 38.4 us -> 38.4 us (level)
  no operation moved by 1% of the time
where the time goes in v8:
time: 38.4 us; the launch traced here: 38.3 us
  Pallas kernels  37.6 us (98%)
  between operations  0.64 us (2%)
    pallas_call x1, Pallas kernels, shards(): pl.pallas_call(functools.partial(kernel, sizes), out_shape=(jax.ShapeDtyp...  36.6 us
    pallas_call x1, Pallas kernels, shards(): pl.pallas_call(last_kernel, out_shape=(jax.ShapeDtypeStruct(wide, bf16),...  1.01 us

profile of v8, /device:TPU:24, one launch (start us, length us, event | category | flops | bytes accessed | tf_op | source)
XLA Modules:
  0.0 38.3 jit_solution(384847526706501554)
XLA Ops:
  0.6 36.6 %hyena.1 = (bf16[256,1024]{1,0:T(8,128)(2,1)S(1)}, bf16[256,1024]{1,0:T(8,128)(2,1)S(1)}, f32[16,1,128]{2,1,0:T(1,128)S(1)}, f32[16,64]{1,0:T(8,128)S(1)}, bf16[1024,64]{1,0:T(8,128)(2,1)S(1)}) custom-call(bf16[1,256,1024]{2,1,0:T(8,128)(2,1)} %x_hbm.1, bf16[1,256,1024]{2,1,0:T(8,128)(2,1)} %d_hbm.1, f32[16,64]{1,0:T(8,128)} %bitcast.5, f32[16,64]{1,0:T(8,128)} %bitcast.6, ...), custom_call_target="tpu_custom_call" | custom-call | tf_op jit(solution)/shard_map/hyena/pallas_call | solution.py:388
  37.3 1.0 %last.1 = (bf16[1,256,1024]{2,1,0:T(8,128)(2,1)}, bf16[1,256,1024]{2,1,0:T(8,128)(2,1)}, f32[16,64]{1,0:T(8,128)}, f32[1,1024]{1,0:T(1,128)}) custom-call(bf16[256,1024]{1,0:T(8,128)(2,1)S(1)} %get-tuple-element.13.y_in, bf16[256,1024]{1,0:T(8,128)(2,1)S(1)} %get-tuple-element.14.z_in, f32[16,1,128]{2,1,0:T(1,128)S(1)} %get-tuple-element.15.final_ref, ...), custom_call_target="tpu_custom_call" | custom-call | tf_op jit(solution)/shard_map/last/pallas_call | solution.py:436

commit v9 on v5

--- a/solution.py
+++ b/solution.py
@@ -159,12 +159,12 @@
         )
 
     def over_peers(body):
-        def turn(step, carried):
-            body(lax.rem(me + step, nctx))
+        def turn(count, carried):
+            body(lax.rem(me + far_first(nctx - 2 - count), nctx))
             return carried
 
         if COMM:
-            lax.fori_loop(1, nctx, turn, 0)
+            lax.fori_loop(0, nctx - 1, turn, 0)
 
     def send_all(kind, send, recv):
         def turn(count, carried):
@@ -301,6 +301,8 @@
     send_all(2, o_send, o_recv)
     o_recv[me] = gradient * scale
 
+    await_sent(0, out_send, out_recv)
+    await_sent(1, back_send, back_recv)
     await_all(1, back_send, back_recv)
     carried_ref[0] = (unpack(back_recv, 0) + states[0] * coefs[2]) * coefs[1]
     carried_ref[1] = (unpack(back_recv, 8) + states[1] * coefs[2]) * coefs[1]
@@ -312,8 +314,7 @@
         z_ref[:, piece] = (zlocal[:, piece] + product).astype(bf16)
 
     by_tiles(finish)
-    for sent in ((0, out_send, out_recv), (1, back_send, back_recv), (2, o_send, o_recv)):
-        await_sent(*sent)
+    await_sent(2, o_send, o_recv)
     if COMM:
         for step in range(1, ndp):
             dp_copy(step, True).wait_send()

time: 37.9 us -> 37.9 us (level)
  no operation moved by 1% of the time
where the time goes in v9:
time: 37.9 us; the launch traced here: 37.8 us
  Pallas kernels  37.2 us (98%)
  between operations  0.64 us (2%)
    pallas_call x1, Pallas kernels, shards(): pl.pallas_call(functools.partial(kernel, sizes), out_shape=(jax.ShapeDtyp...  36.1 us
    pallas_call x1, Pallas kernels, shards(): pl.pallas_call(last_kernel, out_shape=(jax.ShapeDtypeStruct(wide, bf16),...  1.01 us

profile of v9, /device:TPU:24, one launch (start us, length us, event | category | flops | bytes accessed | tf_op | source)
XLA Modules:
  0.0 37.8 jit_solution(4193023402490912573)
XLA Ops:
  0.6 36.1 %hyena.1 = (bf16[256,1024]{1,0:T(8,128)(2,1)S(1)}, bf16[256,1024]{1,0:T(8,128)(2,1)S(1)}, f32[16,1,128]{2,1,0:T(1,128)S(1)}, f32[16,64]{1,0:T(8,128)S(1)}, bf16[1024,64]{1,0:T(8,128)(2,1)S(1)}) custom-call(bf16[1,256,1024]{2,1,0:T(8,128)(2,1)} %x_hbm.1, bf16[1,256,1024]{2,1,0:T(8,128)(2,1)} %d_hbm.1, f32[16,64]{1,0:T(8,128)} %bitcast.5, f32[16,64]{1,0:T(8,128)} %bitcast.6, ...), custom_call_target="tpu_custom_call" | custom-call | tf_op jit(solution)/shard_map/hyena/pallas_call | solution.py:377
  36.8 1.0 %last.1 = (bf16[1,256,1024]{2,1,0:T(8,128)(2,1)}, bf16[1,256,1024]{2,1,0:T(8,128)(2,1)}, f32[16,64]{1,0:T(8,128)}, f32[1,1024]{1,0:T(1,128)}) custom-call(bf16[256,1024]{1,0:T(8,128)(2,1)S(1)} %get-tuple-element.13.y_in, bf16[256,1024]{1,0:T(8,128)(2,1)S(1)} %get-tuple-element.14.z_in, f32[16,1,128]{2,1,0:T(1,128)S(1)} %get-tuple-element.15.final_ref, ...), custom_call_target="tpu_custom_call" | custom-call | tf_op jit(solution)/shard_map/last/pallas_call | solution.py:426
